TPU v7x, 256 devices: a whole 4x4x8 slice. The times are simulated.
256 devices in a mesh: dp: 16 (over y, x_lo, core), pencil: 16 (over x_hi, z).
Axes of the slice: x: 4 (x_hi: 2, x_lo: 2; x = x_hi * 2 + x_lo), y: 4, z: 8, core: 2. Of those that a mesh axis runs over, the one named last changes fastest.
Arguments:
- field_in: bfloat16 [16, 32, 512, 2048], P('dp', None, 'pencil'), may hold values from -6 to 6
- cotangent: bfloat16 [16, 32, 512, 2048], P('dp', None, 'pencil'), may hold values from -3 to 3
- spectral_weight: bfloat16 [128, 128, 2048], P('dp', 'pencil'), may hold values from -0.75 to 0.75
Outputs:
- grad_input: bfloat16 [16, 32, 512, 2048], P('dp', None, 'pencil')
- grad_weight: float32 [128, 128, 2048], P('dp', 'pencil')
All inputs are finite; a program needn't handle non-finite values.
Results may differ from a plain program's by a relative error of at most 0.025.
Values may be sent and summed in bfloat16 or wider, within the bound.
No kernel may reach another device: no remote copies, remote signals or barrier semaphores. Data moves between devices by JAX's collectives and lax.ppermute only.
A program may use at most 128 MiB of HBM per device.

v0:
```python
import math

import jax
import jax.numpy as jnp
import ml_dtypes
import numpy as np
from jax import lax
from jax.experimental import pallas as pl
from jax.experimental.pallas import tpu as pltpu
from jax.sharding import PartitionSpec as P

BF16 = jnp.bfloat16
F32 = jnp.float32
LANES = 128
GROUP = 8
SLABS = 16
CHUNK = 8
TILE = 256
MIB = 1024 * 1024


def row_tables(columns, modes):
    k = np.arange(modes, dtype=np.int64)
    y = np.arange(columns, dtype=np.int64)
    phases = (k[:, None] * y[None, :] % columns).astype(np.float32) * np.float32(
        2.0 * math.pi / columns
    )
    paired = np.stack([np.cos(phases), -np.sin(phases)], axis=0)
    forward = (paired / np.float32(math.sqrt(columns))).reshape(2 * modes, columns)
    factor = np.where(k == 0, 1.0, 2.0).astype(np.float32) / np.float32(math.sqrt(2 * modes))
    inverse = (paired * factor[None, :, None]).reshape(2 * modes, columns)
    return forward.astype(ml_dtypes.bfloat16), inverse.astype(ml_dtypes.bfloat16)


def column_tables(rows, modes):
    j = np.arange(modes, dtype=np.int64)
    f = np.where(j < modes // 2, j, rows - modes + j)
    x = np.arange(rows, dtype=np.int64)
    phases = (f[:, None] * x[None, :] % rows).astype(np.float32) * np.float32(2.0 * math.pi / rows)
    c, s = np.cos(phases), np.sin(phases)
    forward = np.block([[c, s], [-s, c]]) / np.float32(math.sqrt(rows))
    inverse = np.block([[c.T, -s.T], [s.T, c.T]]) / np.float32(math.sqrt(modes))
    return forward.astype(ml_dtypes.bfloat16), inverse.astype(ml_dtypes.bfloat16)


def mode_order(channels, parts=2):
    half = channels // 2
    table = np.zeros((parts * channels * GROUP, parts * channels * GROUP), np.float32)
    for c in range(channels):
        for p in range(parts):
            for k in range(GROUP):
                source = ((c // half * parts + p) * half + c % half) * GROUP + k
                table[source, (k * parts + p) * channels + c] = 1.0
    return table.astype(ml_dtypes.bfloat16)


def dot(a, b):
    return jnp.dot(a, b, preferred_element_type=F32)


def swap_groups(slabs):
    group = lax.broadcasted_iota(jnp.int32, slabs[0].shape, 1) // GROUP
    bit = 1
    while bit < SLABS:
        low = (group & bit) == 0
        out = list(slabs)
        for i in range(SLABS):
            if i & bit:
                continue
            a, b = slabs[i], slabs[i | bit]
            out[i] = jnp.where(low, a, pltpu.roll(b, bit * GROUP, 1))
            out[i | bit] = jnp.where(low, pltpu.roll(a, LANES - bit * GROUP, 1), b)
        slabs = out
        bit *= 2
    return slabs


def pack(spec, out_ref, half):
    rows = out_ref.shape[1]
    for p in range(2):
        slabs = [
            spec[c * rows : (c + 1) * rows, p * LANES : (p + 1) * LANES] for c in range(SLABS)
        ]
        at = (2 * half + p) * LANES
        for d, slab in enumerate(swap_groups(slabs)):
            out_ref[d, :, at : at + LANES] = slab.astype(BF16)


def unpack(in_ref, half):
    parts = []
    for p in range(2):
        at = (2 * half + p) * LANES
        slabs = [in_ref[d, :, at : at + LANES].astype(F32) for d in range(SLABS)]
        parts.append(jnp.concatenate(swap_groups(slabs), axis=0).astype(BF16))
    return jnp.concatenate(parts, axis=1)


def slope(v):
    e = jnp.exp2((-0.5 / math.log(2.0)) * (v * v)).astype(BF16)
    v = v.astype(BF16)

    def c(value):
        return jnp.asarray(value, BF16)

    a = jnp.abs(v)
    t = c(1.0) / (c(1.0) + c(0.3275911 / math.sqrt(2.0)) * a)
    q = c(0.5 * 1.061405429) * t - c(0.5 * 1.453152027)
    q = q * t + c(0.5 * 1.421413741)
    q = q * t - c(0.5 * 0.284496736)
    q = q * t + c(0.5 * 0.254829592)
    g = e * (a * c(1.0 / math.sqrt(2.0 * math.pi)) - q * t)
    return jnp.where(v < c(0.0), -g, c(1.0) + g)


def flat(block):
    return block.reshape(block.shape[0] * block.shape[1], block.shape[-1])


def load(source, target, sem):
    copy = pltpu.make_async_copy(source, target, sem)
    copy.start()
    return copy


def chunk(i):
    return pl.ds(i * CHUNK, CHUNK)


def row_in_kernel(field_hbm, table_hbm, out_ref, field_ref, table_ref, sems):
    chunks = field_ref.shape[0] // CHUNK
    first = load(table_hbm, table_ref, sems.at[chunks])
    copies = [
        load(field_hbm.at[chunk(i)], field_ref.at[chunk(i)], sems.at[i]) for i in range(chunks)
    ]
    first.wait()
    parts = []
    for i in range(chunks):
        copies[i].wait()
        parts.append(dot(flat(field_ref[i * CHUNK : (i + 1) * CHUNK]), table_ref[...]))
    per_half = SLABS // CHUNK
    for h in range(2):
        pack(jnp.concatenate(parts[h * per_half : (h + 1) * per_half], axis=0), out_ref, h)


def middle_kernel(field_ref, cot_ref, back_ref, inv_ref, inv_t_ref, dpre_ref, out_ref):
    rows, columns = field_ref.shape[1:]
    tall = SLABS * rows
    for h in range(2):
        at = slice(h * SLABS, (h + 1) * SLABS)
        back = unpack(back_ref, h)
        cuts = [slice(start, start + TILE) for start in range(0, columns, TILE)]
        total = jnp.zeros((tall, out_ref.shape[2] // 2), F32)
        branch = dot(back, inv_ref[:, cuts[0]])
        held = None
        for n, cut in enumerate(cuts):
            following = dot(back, inv_ref[:, cuts[n + 1]]) if n + 1 < len(cuts) else None
            pre = flat(field_ref[at, :, cut]).astype(F32) + branch
            dpre = (flat(cot_ref[at, :, cut]) * slope(pre)).astype(BF16)
            if held is not None:
                total = total + dot(held, inv_t_ref[cuts[n - 1], :])
            dpre_ref[at, :, cut] = dpre.reshape(SLABS, rows, TILE)
            held, branch = dpre, following
        total = total + dot(held, inv_t_ref[cuts[-1], :])
        pack(total, out_ref, h)


def row_out_kernel(dpre_ref, back_ref, table_ref, out_hbm, out_ref, sems):
    chunks = dpre_ref.shape[0] // CHUNK
    rows, columns = dpre_ref.shape[1:]
    per_half = SLABS // CHUNK
    stores = []
    for h in range(2):
        back = unpack(back_ref, h)
        for n in range(per_half):
            i = h * per_half + n
            left = back[n * CHUNK * rows : (n + 1) * CHUNK * rows]
            at = slice(i * CHUNK, (i + 1) * CHUNK)
            for start in range(0, columns, TILE):
                cut = slice(start, start + TILE)
                value = flat(dpre_ref[at, :, cut]).astype(F32) + dot(left, table_ref[:, cut])
                out_ref[at, :, cut] = value.astype(BF16).reshape(CHUNK, rows, TILE)
            stores.append(load(out_ref.at[chunk(i)], out_hbm.at[chunk(i)], sems.at[i]))
    for copy in stores:
        copy.wait()


def stack_parts(values):
    return jnp.concatenate(
        [
            jnp.concatenate(
                [values[:, (2 * h + p) * LANES : (2 * h + p + 1) * LANES] for h in range(2)], axis=1
            )
            for p in range(2)
        ],
        axis=0,
    )


def lay_parts(result, out_ref):
    rows = out_ref.shape[0]
    for h in range(2):
        for p in range(2):
            at = (2 * h + p) * LANES
            out_ref[:, at : at + LANES] = result[
                p * rows : (p + 1) * rows, h * LANES : (h + 1) * LANES
            ]


def column_kernel(table_ref, in_ref, out_ref):
    lay_parts(dot(table_ref[...], stack_parts(in_ref[...])).astype(BF16), out_ref)


def turn_kernel(
    table_in_ref, in_ref, order_ref, order_t_ref, table_out_ref, sum_ref, weight_hbm,
    dmixed_ref, out_ref,
    weight_ref, same_ref, cross_ref, grad_ref, spec_ref, sems,
):
    rows = dmixed_ref.shape[0]
    total = weight_ref.shape[0]
    width = weight_ref.shape[1]
    piece = 2 * LANES
    loads = [
        load(weight_hbm.at[pl.ds(at, piece)], weight_ref.at[pl.ds(at, piece)], sems.at[n])
        for n, at in enumerate(range(0, total, piece))
    ]
    lay_parts(dot(table_in_ref[...], stack_parts(in_ref[...])).astype(BF16), dmixed_ref)
    dmixed = dot(dmixed_ref[...], order_ref[...])
    lane = lax.broadcasted_iota(jnp.int32, (rows, LANES), 1)
    low = lane < LANES // 2
    real = lane % (LANES // 2) < LANES // 4
    for pair in range(GROUP // 2):
        both = dmixed[:, pair * LANES : (pair + 1) * LANES]
        other = pltpu.roll(both, LANES // 2, 1)
        for i in range(2):
            same = jnp.where(low, both, other) if i == 0 else jnp.where(low, other, both)
            turned = pltpu.roll(same, LANES // 4, 1)
            at = pl.ds(2 * pair + i, rows, stride=GROUP)
            same_ref[at, :] = same
            cross_ref[at, :] = jnp.where(real, turned, -turned)
    for n, at in enumerate(range(0, total, piece)):
        loads[n].wait()
        cut = slice(at, at + piece)
        weight = weight_ref[cut, :]
        copies = width // LANES
        same = jnp.concatenate([same_ref[cut, :].astype(BF16)] * copies, axis=1)
        cross = jnp.concatenate([cross_ref[cut, :].astype(BF16)] * copies, axis=1)
        re = dot(weight * same, sum_ref[...])
        im = dot(weight * cross, sum_ref[...])
        grad_ref[cut, :] = re + pltpu.roll(im, LANES // 4, 1)
    for pair in range(GROUP // 2):
        first = grad_ref[pl.ds(2 * pair, rows, stride=GROUP), :]
        second = grad_ref[pl.ds(2 * pair + 1, rows, stride=GROUP), :]
        both = jnp.where(low, first, pltpu.roll(second, LANES // 2, 1))
        spec_ref[:, pair * LANES : (pair + 1) * LANES] = both.astype(BF16)
    dspec = dot(spec_ref[...], order_t_ref[...]).astype(BF16)
    lay_parts(dot(table_out_ref[...], stack_parts(dspec)).astype(BF16), out_ref)


def weight_kernel(in_ref, out_ref):
    modes, channels = in_ref.shape[0], in_ref.shape[2]
    zero = jnp.zeros((2 * channels, 2 * channels), F32)
    for j in range(modes):
        for pair in range(GROUP // 2):
            blocks = []
            for i in range(2):
                w = in_ref[j, 2 * pair + i].astype(F32)
                turned = jnp.concatenate([-w[:, channels:], w[:, :channels]], axis=1)
                block = jnp.concatenate([w, turned], axis=0)
                blocks.append(
                    jnp.concatenate([block, zero] if i == 0 else [zero, block], axis=1)
                )
            out_ref[pair, :, j * LANES : (j + 1) * LANES] = jnp.concatenate(blocks, axis=0).astype(
                BF16
            )


def own_row(shape, axis):
    return lax.broadcasted_iota(jnp.int32, shape, axis) % GROUP


def mix_kernel(in_ref, weight_ref, order_ref, order_t_ref, out_ref):
    values = dot(in_ref[...], order_ref[...]).astype(BF16)
    rows = values.shape[0]
    own = own_row((rows, LANES), 0)
    pieces = []
    for pair in range(GROUP // 2):
        left = values[:, pair * LANES : (pair + 1) * LANES]
        total = jnp.zeros((rows, LANES), F32)
        for j in range(GROUP):
            weight = weight_ref[pair, :, j * LANES : (j + 1) * LANES]
            term = dot(left, weight)
            total = jnp.where(own == j, term, total)
        pieces.append(total.astype(BF16))
    mixed = jnp.concatenate(pieces, axis=1)
    out_ref[...] = dot(mixed, order_t_ref[...]).astype(BF16)


def grad_kernel(spec_ref, dmixed_ref, order_ref, out_ref):
    spec = dot(spec_ref[...], order_ref[...])
    dmixed = dot(dmixed_ref[...], order_ref[...]).astype(BF16)
    rows = spec.shape[0]
    channels = out_ref.shape[2]
    own = own_row((LANES, rows), 1)
    for pair in range(GROUP // 2):
        left = spec[:, pair * LANES : (pair + 1) * LANES].T
        right = dmixed[:, pair * LANES : (pair + 1) * LANES]
        for j in range(GROUP):
            outer = dot(jnp.where(own == j, left, 0.0).astype(BF16), right)
            for i in range(2):
                at = 2 * channels * i
                re = outer[at : at + channels, at : at + 2 * channels]
                im = outer[at + channels : at + 2 * channels, at : at + 2 * channels]
                turned = jnp.concatenate([im[:, channels:], -im[:, :channels]], axis=1)
                out_ref[j, 2 * pair + i] = re + turned


def shaped(shape, dtype=BF16):
    return jax.ShapeDtypeStruct(shape, dtype)


def call(kernel, out, name, vmem=16, **kw):
    return pl.pallas_call(
        kernel,
        out_shape=out,
        name=name,
        compiler_params=pltpu.CompilerParams(vmem_limit_bytes=vmem * MIB),
        **kw,
    )


ANY = pl.BlockSpec(memory_space=pl.ANY)
WHOLE = pl.BlockSpec(memory_space=pltpu.VMEM)


def buffers(*shapes):
    return [pltpu.VMEM(shape, BF16) for shape in shapes]


def sems(count):
    return pltpu.SemaphoreType.DMA((count,))


def across(values, axis):
    return lax.all_to_all(values, axis, split_axis=0, concat_axis=0, tiled=True)


def local(field_in, cotangent, spectral_weight):
    channels, rows_here, columns = field_in.shape[1:]
    pencils = lax.axis_size("pencil")
    modes_y = spectral_weight.shape[1] * pencils
    modes_x = spectral_weight.shape[0] * lax.axis_size("dp")
    height = rows_here * pencils
    wide = 4 * LANES
    chunks = channels // CHUNK
    row_fwd_t, row_inv = row_tables(columns, modes_y)
    col_fwd, col_inv = column_tables(height, modes_x)
    order = mode_order(channels)
    lane = np.arange(spectral_weight.shape[2])
    summed = (lane[:, None] // (2 * channels) == np.arange(LANES)[None, :]).astype(
        ml_dtypes.bfloat16
    )
    field = field_in[0]
    cot = cotangent[0]
    field_shape = field.shape
    sent_shape = (SLABS, rows_here, wide)
    tall = (columns, 2 * modes_y)

    def turned(table):
        return jnp.asarray(np.ascontiguousarray(table.T))

    def column(table, values, name):
        return call(column_kernel, shaped((table.shape[0] // 2, wide)), name)(table, values)

    gathered = lax.all_gather(spectral_weight, "dp", axis=0, tiled=True)
    weights = call(
        weight_kernel, shaped((GROUP // 2, LANES, GROUP * LANES)), "weight_blocks"
    )(spectral_weight.reshape(GROUP, GROUP, channels, 2 * channels))
    order_in, order_out = jnp.asarray(order), turned(order)

    sent = call(
        row_in_kernel, shaped(sent_shape), "row_in", 60,
        in_specs=[ANY] * 2, out_specs=WHOLE,
        scratch_shapes=buffers(field_shape, tall) + [sems(chunks + 1)],
    )(field, turned(row_fwd_t))
    arrived = across(sent, "pencil").reshape(height, wide)
    spectrum = across(column(jnp.asarray(col_fwd), arrived, "column_in"), "dp")
    mixed = across(
        call(mix_kernel, shaped((modes_x, wide)), "mix")(spectrum, weights, order_in, order_out),
        "dp",
    )
    back = across(column(jnp.asarray(col_inv), mixed, "column_out"), "pencil")
    dpre, sent = call(
        middle_kernel, [shaped(field_shape), shaped(sent_shape)], "middle", 16,
        in_specs=[WHOLE] * 5, out_specs=[WHOLE] * 2,
    )(field, cot, back.reshape(sent_shape), jnp.asarray(row_inv), turned(row_inv))
    arrived = across(sent, "pencil").reshape(height, wide)
    modes = modes_x * GROUP
    dmixed, sent = call(
        turn_kernel, [shaped((modes_x, wide)), shaped((height, wide))], "turn", 28,
        in_specs=[WHOLE] * 6 + [ANY], out_specs=[WHOLE] * 2,
        scratch_shapes=[
            pltpu.VMEM((modes, spectral_weight.shape[2]), BF16),
            pltpu.VMEM((modes, LANES), F32),
            pltpu.VMEM((modes, LANES), F32),
            pltpu.VMEM((modes, LANES), F32),
            pltpu.VMEM((modes_x, wide), BF16),
            sems(modes // (2 * LANES)),
        ],
    )(
        turned(col_inv), arrived, order_in, order_out, turned(col_fwd), jnp.asarray(summed),
        gathered.reshape(modes, spectral_weight.shape[2]),
    )
    back = across(sent, "pencil").reshape(sent_shape)
    grad_weight = call(
        grad_kernel, shaped((GROUP, GROUP, channels, 2 * channels), F32), "weight_grad"
    )(spectrum, across(dmixed, "dp"), order_in)
    grad_input = call(
        row_out_kernel, shaped(field_shape), "row_out", 16,
        in_specs=[WHOLE] * 3, out_specs=ANY,
        scratch_shapes=buffers(field_shape) + [sems(chunks)],
    )(dpre, back, jnp.asarray(row_fwd_t))
    return (grad_input[None], grad_weight.reshape(spectral_weight.shape))


def solution(mesh):
    return jax.shard_map(
        local,
        mesh=mesh,
        in_specs=(
            P("dp", None, "pencil", None),
            P("dp", None, "pencil", None),
            P("dp", "pencil", None),
        ),
        out_specs=(P("dp", None, "pencil", None), P("dp", "pencil", None)),
        check_vma=False,
    )
```

profile of v0, /device:TPU:32, one launch (start us, length us, event | category | flops | bytes accessed | tf_op | source)
XLA Modules:
  0.0 175.4 jit_solution(8053873213583309324)
XLA Ops:
  7.2 0.0 copy-start.14
  7.2 0.0 all-gather.2.cloned.1.call-start
  7.2 0.7 all-gather.2.cloned.1.call-update
  7.9 0.0 copy-start.15
  7.9 0.0 copy-start.1
  7.9 0.0 copy-start.6
  7.9 5.8 %row_in.1 = bf16[16,32,512]{2,1,0:T(8,128)(2,1)} custom-call(bf16[32,32,2048]{2,1,0:T(8,128)(2,1)} %bitcast.16, bf16[2048,256]{1,0:T(8,128)(2,1)} %constant.24.clone.table_hbm), custom_call_target="tpu_custom_call" | custom-call | tf_op jit(solution)/shard_map/row_in/pallas_call | solution.py:380
  13.8 0.0 copy-start.13
  13.8 27.6 %all_to_all.61 = bf16[16,32,512]{2,1,0:T(8,128)(2,1)S(1)} all-to-all(bf16[16,32,512]{2,1,0:T(8,128)(2,1)} %row_in.1), channel_id=1, replica_groups=mesh['dp'=16,'pencil'=16] {'pencil'}, dimensions={0} | all-to-all | bytes 1048576 | tf_op jit(solution)/shard_map/all_to_all | solution.py:344
  41.3 0.0 copy-done.14
  41.3 1.0 column_in.1
  42.3 4.6 %all-to-all-start.1 = ((bf16[16,8,512]{2,1,0:T(8,128)(2,1)}), bf16[16,8,512]{2,1,0:T(8,128)(2,1)S(1)}, u32[]{:S(2)}, u32[]{:S(2)}) async-start(bf16[16,8,512]{2,1,0:T(8,128)(2,1)} %bitcast.3), calls=%async_computation.1 | async-start | bytes 262144 | tf_op jit(solution)/shard_map/all_to_all | solution.py:344
  46.9 0.0 copy-done.15
  46.9 0.5 reshape.34.in_ref
  47.4 2.1 %weight_blocks.1.weight_ref = bf16[4,128,1024]{2,1,0:T(8,128)(2,1)S(1)} custom-call(bf16[8,8,32,64]{3,2,1,0:T(8,128)(2,1)S(1)} %reshape.34.in_ref), custom_call_target="tpu_custom_call" | custom-call | tf_op jit(solution)/shard_map/weight_blocks/pallas_call | solution.py:375
  49.5 5.4 %all-to-all-done.1 = bf16[16,8,512]{2,1,0:T(8,128)(2,1)S(1)} async-done(((bf16[16,8,512]{2,1,0:T(8,128)(2,1)}), bf16[16,8,512]{2,1,0:T(8,128)(2,1)S(1)}, u32[]{:S(2)}, u32[]{:S(2)}) %all-to-all-start.1) | async-done | bytes 131104 | tf_op jit(solution)/shard_map/all_to_all | solution.py:344
  54.9 0.0 copy-start
  54.9 0.0 copy-done.1
  54.9 0.0 copy-done.6
  54.9 0.8 mix.1
  55.7 9.4 %all_to_all.62 = bf16[16,8,512]{2,1,0:T(8,128)(2,1)S(1)} all-to-all(bf16[16,8,512]{2,1,0:T(8,128)(2,1)S(1)} %bitcast.27), channel_id=1, replica_groups=mesh['dp'=16,'pencil'=16] {'dp'}, dimensions={0} | all-to-all | bytes 262144 | tf_op jit(solution)/shard_map/all_to_all | solution.py:344
  65.2 0.0 copy-done.13
  65.2 0.3 column_out.1
  65.5 22.1 %all_to_all.63.back_ref = bf16[16,32,512]{2,1,0:T(8,128)(2,1)S(1)} all-to-all(bf16[16,32,512]{2,1,0:T(8,128)(2,1)S(1)} %bitcast.22), channel_id=1, replica_groups=mesh['dp'=16,'pencil'=16] {'pencil'}, dimensions={0} | all-to-all | bytes 1048576 | tf_op jit(solution)/shard_map/all_to_all | solution.py:344
  87.6 0.0 copy-done
  87.6 0.0 copy-start.3
  87.6 2.2 %copy-done.3 = bf16[1,32,32,2048]{3,2,1,0:T(8,128)(2,1)S(1)} copy-done((bf16[1,32,32,2048]{3,2,1,0:T(8,128)(2,1)S(1)}, bf16[1,32,32,2048]{3,2,1,0:T(8,128)(2,1)}, u32[]{:S(2)}) %copy-start.3) | copy-done | bytes 4194328
  89.8 0.0 copy-start.8
  89.8 1.2 copy-done.8
  91.0 1.2 copy-done.9
  92.3 0.0 copy-start.10
  92.3 6.5 %middle.1 = (bf16[32,32,2048]{2,1,0:T(8,128)(2,1)S(1)}, bf16[16,32,512]{2,1,0:T(8,128)(2,1)S(1)}) custom-call(bf16[32,32,2048]{2,1,0:T(8,128)(2,1)S(1)} %bitcast.17, bf16[32,32,2048]{2,1,0:T(8,128)(2,1)S(1)} %bitcast.19, bf16[16,32,512]{2,1,0:T(8,128)(2,1)S(1)} %all_to_all.63.back_ref, bf16[256,2048]{1,0:T(8,128)(2,1)S(1)} %copy-done.9, ...), custom_call_target="tpu_custom_call" | custom-call | tf_op jit(solution)/shard_map/middle/pallas_call | solution.py:392
  98.8 0.0 copy-start.4
  98.8 2.0 %copy-done.4 = bf16[32,32,2048]{2,1,0:T(8,128)(2,1)} copy-done((bf16[32,32,2048]{2,1,0:T(8,128)(2,1)}, bf16[32,32,2048]{2,1,0:T(8,128)(2,1)S(1)}, u32[]{:S(2)}) %copy-start.4) | copy-done | bytes 4194328
  100.8 21.4 %all_to_all.64 = bf16[16,32,512]{2,1,0:T(8,128)(2,1)S(1)} all-to-all(bf16[16,32,512]{2,1,0:T(8,128)(2,1)S(1)} %get-tuple-element.7), channel_id=1, replica_groups=mesh['dp'=16,'pencil'=16] {'pencil'}, dimensions={0} | all-to-all | bytes 1048576 | tf_op jit(solution)/shard_map/all_to_all | solution.py:344
  122.2 0.0 copy-done.10
  122.2 0.0 copy-done.11
  122.2 2.2 %copy-done.2 = bf16[128,8,2048]{2,1,0:T(8,128)(2,1)S(1)} copy-done((bf16[128,8,2048]{2,1,0:T(8,128)(2,1)S(1)}, bf16[128,8,2048]{2,1,0:T(8,128)(2,1)}, u32[]{:S(2)}) %copy-start.2) | copy-done | bytes 4194328
  124.4 1.0 copy-done.12
  125.4 5.4 %turn.1 = (bf16[128,512]{1,0:T(8,128)(2,1)S(1)}, bf16[512,512]{1,0:T(8,128)(2,1)}) custom-call(bf16[256,1024]{1,0:T(8,128)(2,1)S(1)} %copy-done.12, bf16[512,512]{1,0:T(8,128)(2,1)S(1)} %bitcast.20, bf16[512,512]{1,0:T(8,128)(2,1)S(1)} %copy-done.1, bf16[512,512]{1,0:T(8,128)(2,1)S(1)} %copy-done.6, bf16[1024,256]{1,0:T(8,128)(2,1)S(1)} %copy-done.11, ...), custom_call_target="tpu_custom_call" | custom-call | tf_op jit(solution)/shard_map/turn/pallas_call | solution.py:398
  130.8 9.5 %all_to_all.65 = bf16[16,8,512]{2,1,0:T(8,128)(2,1)S(1)} all-to-all(bf16[16,8,512]{2,1,0:T(8,128)(2,1)S(1)} %bitcast.28), channel_id=1, replica_groups=mesh['dp'=16,'pencil'=16] {'dp'}, dimensions={0} | all-to-all | bytes 262144 | tf_op jit(solution)/shard_map/all_to_all | solution.py:344
  140.3 5.6 %all-to-all-start.5 = ((bf16[16,32,512]{2,1,0:T(8,128)(2,1)}), bf16[16,32,512]{2,1,0:T(8,128)(2,1)S(1)}, u32[]{:S(2)}, u32[]{:S(2)}) async-start(bf16[16,32,512]{2,1,0:T(8,128)(2,1)} %bitcast.10), calls=%async_computation.5 | async-start | bytes 1048576 | tf_op jit(solution)/shard_map/all_to_all | solution.py:344
  145.9 2.0 %weight_grad.1 = f32[8,8,32,64]{3,2,1,0:T(8,128)S(1)} custom-call(bf16[128,512]{1,0:T(8,128)(2,1)S(1)} %bitcast.24, bf16[128,512]{1,0:T(8,128)(2,1)S(1)} %bitcast.25, bf16[512,512]{1,0:T(8,128)(2,1)S(1)} %copy-done.1), custom_call_target="tpu_custom_call" | custom-call | tf_op jit(solution)/shard_map/weight_grad/pallas_call | solution.py:414
  147.9 1.2 reshape.37
  149.0 13.2 %all-to-all-done.5.back_ref = bf16[16,32,512]{2,1,0:T(8,128)(2,1)S(1)} async-done(((bf16[16,32,512]{2,1,0:T(8,128)(2,1)}), bf16[16,32,512]{2,1,0:T(8,128)(2,1)S(1)}, u32[]{:S(2)}, u32[]{:S(2)}) %all-to-all-start.5) | async-done | bytes 524320 | tf_op jit(solution)/shard_map/all_to_all | solution.py:344
  162.2 2.2 %copy-done.5 = bf16[32,32,2048]{2,1,0:T(8,128)(2,1)S(1)} copy-done((bf16[32,32,2048]{2,1,0:T(8,128)(2,1)S(1)}, bf16[32,32,2048]{2,1,0:T(8,128)(2,1)}, u32[]{:S(2)}) %copy-start.5) | copy-done | bytes 4194328
  164.4 1.2 copy-done.7
  165.7 2.9 %row_out.1 = bf16[32,32,2048]{2,1,0:T(8,128)(2,1)} custom-call(bf16[32,32,2048]{2,1,0:T(8,128)(2,1)S(1)} %copy-done.5, bf16[16,32,512]{2,1,0:T(8,128)(2,1)S(1)} %all-to-all-done.5.back_ref, bf16[256,2048]{1,0:T(8,128)(2,1)S(1)} %copy-done.7), custom_call_target="tpu_custom_call" | custom-call | tf_op jit(solution)/shard_map/row_out/pallas_call | solution.py:417
  (7 shorter events, 0.0 us)
Async XLA Ops:
  7.2 34.2 %copy-start.14 = (bf16[256,1024]{1,0:T(8,128)(2,1)S(1)}, bf16[256,1024]{1,0:T(8,128)(2,1)}, u32[]{:S(2)}) copy-start(bf16[256,1024]{1,0:T(8,128)(2,1)} %constant.25.clone.table_ref) | copy-start | bytes 1572868
  7.2 115.0 %all-gather.2.cloned.1.call-start = ((), (), s32[]{:S(2)}) async-start(), calls=%async_computation.7 | async-start | bytes 4456448 | tf_op jit(solution)/shard_map/all_gather | solution.py:374
  7.9 39.0 %copy-start.15 = (bf16[8,8,2048]{2,1,0:T(8,128)(2,1)S(1)}, bf16[8,8,2048]{2,1,0:T(8,128)(2,1)}, u32[]{:S(2)}) copy-start(bf16[8,8,2048]{2,1,0:T(8,128)(2,1)} %param.16) | copy-start | bytes 786436
  7.9 47.0 %copy-start.1 = (bf16[512,512]{1,0:T(8,128)(2,1)S(1)}, bf16[512,512]{1,0:T(8,128)(2,1)}, u32[]{:S(2)}) copy-start(bf16[512,512]{1,0:T(8,128)(2,1)} %constant.22.clone.order_ref) | copy-start | bytes 1572868
  7.9 47.0 %copy-start.6 = (bf16[512,512]{1,0:T(8,128)(2,1)S(1)}, bf16[512,512]{1,0:T(8,128)(2,1)}, u32[]{:S(2)}) copy-start(bf16[512,512]{1,0:T(8,128)(2,1)} %constant.23.clone.order_t_ref) | copy-start | bytes 1572868
  13.8 51.4 %copy-start.13 = (bf16[1024,256]{1,0:T(8,128)(2,1)S(1)}, bf16[1024,256]{1,0:T(8,128)(2,1)}, u32[]{:S(2)}) copy-start(bf16[1024,256]{1,0:T(8,128)(2,1)} %constant.26.clone.table_ref) | copy-start | bytes 1572868
  42.3 12.6 %all-to-all-start.1 = ((bf16[16,8,512]{2,1,0:T(8,128)(2,1)}), bf16[16,8,512]{2,1,0:T(8,128)(2,1)S(1)}, u32[]{:S(2)}, u32[]{:S(2)}) async-start(bf16[16,8,512]{2,1,0:T(8,128)(2,1)} %bitcast.3), calls=%async_computation.1 | async-start | bytes 262144 | tf_op jit(solution)/shard_map/all_to_all | solution.py:344
  54.9 32.7 %copy-start = (bf16[1,32,32,2048]{3,2,1,0:T(8,128)(2,1)S(1)}, bf16[1,32,32,2048]{3,2,1,0:T(8,128)(2,1)}, u32[]{:S(2)}) copy-start(bf16[1,32,32,2048]{3,2,1,0:T(8,128)(2,1)} %param.14) | copy-start | bytes 12582916
  87.6 2.2 %copy-start.3 = (bf16[1,32,32,2048]{3,2,1,0:T(8,128)(2,1)S(1)}, bf16[1,32,32,2048]{3,2,1,0:T(8,128)(2,1)}, u32[]{:S(2)}) copy-start(bf16[1,32,32,2048]{3,2,1,0:T(8,128)(2,1)} %param.15) | copy-start | bytes 12582916
  89.8 1.2 copy-start.8
  91.0 1.2 copy-start.9
  92.3 29.9 %copy-start.10 = (bf16[2048,128]{1,0:T(8,128)(2,1)S(1)}, bf16[2048,128]{1,0:T(8,128)(2,1)}, u32[]{:S(2)}) copy-start(bf16[2048,128]{1,0:T(8,128)(2,1)} %constant.31.clone.sum_ref) | copy-start | bytes 1572868
  92.3 29.9 %copy-start.11 = (bf16[1024,256]{1,0:T(8,128)(2,1)S(1)}, bf16[1024,256]{1,0:T(8,128)(2,1)}, u32[]{:S(2)}) copy-start(bf16[1024,256]{1,0:T(8,128)(2,1)} %constant.30.clone.table_out_ref) | copy-start | bytes 1572868
  98.8 2.0 %copy-start.4 = (bf16[32,32,2048]{2,1,0:T(8,128)(2,1)}, bf16[32,32,2048]{2,1,0:T(8,128)(2,1)S(1)}, u32[]{:S(2)}) copy-start(bf16[32,32,2048]{2,1,0:T(8,128)(2,1)S(1)} %get-tuple-element.6.dpre_ref) | copy-start | bytes 12582916
  122.2 2.2 %copy-start.2 = (bf16[128,8,2048]{2,1,0:T(8,128)(2,1)S(1)}, bf16[128,8,2048]{2,1,0:T(8,128)(2,1)}, u32[]{:S(2)}) copy-start(bf16[128,8,2048]{2,1,0:T(8,128)(2,1)} %all-gather.2.cloned.1.call-done) | copy-start | bytes 12582916
  124.4 1.0 copy-start.12
  140.3 21.9 %all-to-all-start.5 = ((bf16[16,32,512]{2,1,0:T(8,128)(2,1)}), bf16[16,32,512]{2,1,0:T(8,128)(2,1)S(1)}, u32[]{:S(2)}, u32[]{:S(2)}) async-start(bf16[16,32,512]{2,1,0:T(8,128)(2,1)} %bitcast.10), calls=%async_computation.5 | async-start | bytes 1048576 | tf_op jit(solution)/shard_map/all_to_all | solution.py:344
  162.2 2.2 %copy-start.5 = (bf16[32,32,2048]{2,1,0:T(8,128)(2,1)S(1)}, bf16[32,32,2048]{2,1,0:T(8,128)(2,1)}, u32[]{:S(2)}) copy-start(bf16[32,32,2048]{2,1,0:T(8,128)(2,1)} %copy-done.4) | copy-start | bytes 12582916
  164.4 1.2 copy-start.7
Sparse Core Ops, SparseCore 0:
  9.9 47.9 all-gather.1
where the time goes:
time: 176 us; the launch traced here: 175 us
  blocking collectives  90 us (51%)
  Pallas kernels  26.7 us (15%)
  waiting for transfers between devices  19.3 us (11%)
  local copies, waits for them, and re-layouts  15 us (9%)
  between operations  14.2 us (8%)
  starting transfers between devices  10.2 us (6%)
    all_to_all x5, blocking collectives, across(): return lax.all_to_all(values, axis, split_axis=0, concat_axis=0, tiled=True)  90 us
    all_to_all x2, waiting for transfers between devices, across(): return lax.all_to_all(values, axis, split_axis=0, concat_axis=0, tiled=True)  18.6 us
    unnamed x32, local copies, waits for them, and re-layouts  13.3 us
    all_to_all x2, starting transfers between devices, across(): return lax.all_to_all(values, axis, split_axis=0, concat_axis=0, tiled=True)  10.2 us
    pallas_call x1, Pallas kernels, local(): call(middle_kernel, [shaped(field_shape), shaped(sent_shape)], 'middle',...  6.53 us
    pallas_call x1, Pallas kernels, local(): call(row_in_kernel, shaped(sent_shape), 'row_in', 60, in_specs=[ANY] * 2,...  5.81 us
    pallas_call x1, Pallas kernels, local(): call(turn_kernel, [shaped((modes_x, wide)), shaped((height, wide))], 'tur...  5.38 us
  transfers between devices with their start and end apart: 3, of which 2 were waited for; matrix products, arithmetic and copies ran while one was open for 1% of the time, Pallas kernels for 11%

commit v1 on v0

--- a/solution.py
+++ b/solution.py
@@ -16,6 +16,7 @@
 SLABS = 16
 CHUNK = 8
 TILE = 256
+SPANS = 2
 MIB = 1024 * 1024
 
 
@@ -126,12 +127,15 @@
     return pl.ds(i * CHUNK, CHUNK)
 
 
-def row_in_kernel(field_hbm, table_hbm, out_ref, field_ref, table_ref, sems):
+def row_in_kernel(
+    field_hbm, table_hbm, weight_hbm, out_ref, passed_hbm, field_ref, table_ref, sems
+):
     chunks = field_ref.shape[0] // CHUNK
     first = load(table_hbm, table_ref, sems.at[chunks])
     copies = [
         load(field_hbm.at[chunk(i)], field_ref.at[chunk(i)], sems.at[i]) for i in range(chunks)
     ]
+    passed = load(weight_hbm, passed_hbm, sems.at[chunks + 1])
     first.wait()
     parts = []
     for i in range(chunks):
@@ -140,46 +144,89 @@
     per_half = SLABS // CHUNK
     for h in range(2):
         pack(jnp.concatenate(parts[h * per_half : (h + 1) * per_half], axis=0), out_ref, h)
-
-
-def middle_kernel(field_ref, cot_ref, back_ref, inv_ref, inv_t_ref, dpre_ref, out_ref):
+    passed.wait()
+
+
+def middle_kernel(
+    field_hbm, cot_hbm, back_ref, inv_hbm, inv_t_hbm, dpre_hbm, out_ref,
+    field_ref, cot_ref, inv_ref, inv_t_ref, dpre_ref, sems, sent_sems,
+):
     rows, columns = field_ref.shape[1:]
+    span = columns // SPANS
+    inv_load = load(inv_hbm, inv_ref, sems.at[0])
+    inv_t_load = None
+    loads = []
+    for h in range(2):
+        for n in range(SPANS):
+            at = (pl.ds(h * SLABS, SLABS), slice(None), pl.ds(n * span, span))
+            slot = 2 + 2 * (h * SPANS + n)
+            loads.append(
+                (
+                    load(field_hbm.at[at], field_ref.at[at], sems.at[slot]),
+                    load(cot_hbm.at[at], cot_ref.at[at], sems.at[slot + 1]),
+                )
+            )
+            if inv_t_load is None:
+                inv_t_load = load(inv_t_hbm, inv_t_ref, sems.at[1])
     tall = SLABS * rows
+    stores = []
     for h in range(2):
         at = slice(h * SLABS, (h + 1) * SLABS)
         back = unpack(back_ref, h)
-        cuts = [slice(start, start + TILE) for start in range(0, columns, TILE)]
         total = jnp.zeros((tall, out_ref.shape[2] // 2), F32)
-        branch = dot(back, inv_ref[:, cuts[0]])
-        held = None
-        for n, cut in enumerate(cuts):
-            following = dot(back, inv_ref[:, cuts[n + 1]]) if n + 1 < len(cuts) else None
-            pre = flat(field_ref[at, :, cut]).astype(F32) + branch
-            dpre = (flat(cot_ref[at, :, cut]) * slope(pre)).astype(BF16)
-            if held is not None:
-                total = total + dot(held, inv_t_ref[cuts[n - 1], :])
-            dpre_ref[at, :, cut] = dpre.reshape(SLABS, rows, TILE)
-            held, branch = dpre, following
-        total = total + dot(held, inv_t_ref[cuts[-1], :])
+        if h == 0:
+            inv_load.wait()
+        for n in range(SPANS):
+            for copy in loads[h * SPANS + n]:
+                copy.wait()
+            if h == 0 and n == 0:
+                inv_t_load.wait()
+            cuts = [slice(y, y + TILE) for y in range(n * span, (n + 1) * span, TILE)]
+            branch = dot(back, inv_ref[:, cuts[0]])
+            held = None
+            for m, cut in enumerate(cuts):
+                following = dot(back, inv_ref[:, cuts[m + 1]]) if m + 1 < len(cuts) else None
+                pre = flat(field_ref[at, :, cut]).astype(F32) + branch
+                dpre = (flat(cot_ref[at, :, cut]) * slope(pre)).astype(BF16)
+                if held is not None:
+                    total = total + dot(held, inv_t_ref[cuts[m - 1], :])
+                dpre_ref[at, :, cut] = dpre.reshape(SLABS, rows, TILE)
+                held, branch = dpre, following
+            total = total + dot(held, inv_t_ref[cuts[-1], :])
+            place = (pl.ds(h * SLABS, SLABS), slice(None), pl.ds(n * span, span))
+            stores.append(
+                load(dpre_ref.at[place], dpre_hbm.at[place], sent_sems.at[h * SPANS + n])
+            )
         pack(total, out_ref, h)
-
-
-def row_out_kernel(dpre_ref, back_ref, table_ref, out_hbm, out_ref, sems):
+    for copy in stores:
+        copy.wait()
+
+
+def row_out_kernel(
+    dpre_hbm, back_ref, table_hbm, out_hbm, dpre_ref, table_ref, out_ref, sems, sent_sems
+):
     chunks = dpre_ref.shape[0] // CHUNK
     rows, columns = dpre_ref.shape[1:]
     per_half = SLABS // CHUNK
+    table_load = load(table_hbm, table_ref, sems.at[chunks])
+    loads = [
+        load(dpre_hbm.at[chunk(i)], dpre_ref.at[chunk(i)], sems.at[i]) for i in range(chunks)
+    ]
     stores = []
     for h in range(2):
         back = unpack(back_ref, h)
+        if h == 0:
+            table_load.wait()
         for n in range(per_half):
             i = h * per_half + n
+            loads[i].wait()
             left = back[n * CHUNK * rows : (n + 1) * CHUNK * rows]
             at = slice(i * CHUNK, (i + 1) * CHUNK)
             for start in range(0, columns, TILE):
                 cut = slice(start, start + TILE)
                 value = flat(dpre_ref[at, :, cut]).astype(F32) + dot(left, table_ref[:, cut])
                 out_ref[at, :, cut] = value.astype(BF16).reshape(CHUNK, rows, TILE)
-            stores.append(load(out_ref.at[chunk(i)], out_hbm.at[chunk(i)], sems.at[i]))
+            stores.append(load(out_ref.at[chunk(i)], out_hbm.at[chunk(i)], sent_sems.at[i]))
     for copy in stores:
         copy.wait()
 
@@ -211,8 +258,7 @@
 
 
 def turn_kernel(
-    table_in_ref, in_ref, order_ref, order_t_ref, table_out_ref, sum_ref, weight_hbm,
-    dmixed_ref, out_ref,
+    dmixed_ref, order_ref, order_t_ref, table_out_ref, sum_ref, weight_hbm, out_ref,
     weight_ref, same_ref, cross_ref, grad_ref, spec_ref, sems,
 ):
     rows = dmixed_ref.shape[0]
@@ -223,7 +269,6 @@
         load(weight_hbm.at[pl.ds(at, piece)], weight_ref.at[pl.ds(at, piece)], sems.at[n])
         for n, at in enumerate(range(0, total, piece))
     ]
-    lay_parts(dot(table_in_ref[...], stack_parts(in_ref[...])).astype(BF16), dmixed_ref)
     dmixed = dot(dmixed_ref[...], order_ref[...])
     lane = lax.broadcasted_iota(jnp.int32, (rows, LANES), 1)
     low = lane < LANES // 2
@@ -295,7 +340,7 @@
     out_ref[...] = dot(mixed, order_t_ref[...]).astype(BF16)
 
 
-def grad_kernel(spec_ref, dmixed_ref, order_ref, out_ref):
+def grad_kernel(spec_ref, dmixed_ref, order_ref, after_hbm, out_ref):
     spec = dot(spec_ref[...], order_ref[...])
     dmixed = dot(dmixed_ref[...], order_ref[...]).astype(BF16)
     rows = spec.shape[0]
@@ -328,7 +373,7 @@
     )
 
 
-ANY = pl.BlockSpec(memory_space=pl.ANY)
+HBM = pl.BlockSpec(memory_space=pltpu.HBM)
 WHOLE = pl.BlockSpec(memory_space=pltpu.VMEM)
 
 
@@ -363,7 +408,7 @@
     cot = cotangent[0]
     field_shape = field.shape
     sent_shape = (SLABS, rows_here, wide)
-    tall = (columns, 2 * modes_y)
+    narrow, tall = (2 * modes_y, columns), (columns, 2 * modes_y)
 
     def turned(table):
         return jnp.asarray(np.ascontiguousarray(table.T))
@@ -371,17 +416,17 @@
     def column(table, values, name):
         return call(column_kernel, shaped((table.shape[0] // 2, wide)), name)(table, values)
 
-    gathered = lax.all_gather(spectral_weight, "dp", axis=0, tiled=True)
     weights = call(
         weight_kernel, shaped((GROUP // 2, LANES, GROUP * LANES)), "weight_blocks"
     )(spectral_weight.reshape(GROUP, GROUP, channels, 2 * channels))
     order_in, order_out = jnp.asarray(order), turned(order)
 
-    sent = call(
-        row_in_kernel, shaped(sent_shape), "row_in", 60,
-        in_specs=[ANY] * 2, out_specs=WHOLE,
-        scratch_shapes=buffers(field_shape, tall) + [sems(chunks + 1)],
-    )(field, turned(row_fwd_t))
+    sent, passed = call(
+        row_in_kernel, [shaped(sent_shape), shaped(spectral_weight.shape)], "row_in", 60,
+        in_specs=[HBM] * 3, out_specs=[WHOLE, HBM],
+        scratch_shapes=buffers(field_shape, tall) + [sems(chunks + 2)],
+    )(field, turned(row_fwd_t), spectral_weight)
+    gathered = lax.all_gather(passed, "dp", axis=0, tiled=True)
     arrived = across(sent, "pencil").reshape(height, wide)
     spectrum = across(column(jnp.asarray(col_fwd), arrived, "column_in"), "dp")
     mixed = across(
@@ -390,14 +435,18 @@
     )
     back = across(column(jnp.asarray(col_inv), mixed, "column_out"), "pencil")
     dpre, sent = call(
-        middle_kernel, [shaped(field_shape), shaped(sent_shape)], "middle", 16,
-        in_specs=[WHOLE] * 5, out_specs=[WHOLE] * 2,
+        middle_kernel, [shaped(field_shape), shaped(sent_shape)], "middle", 60,
+        in_specs=[HBM, HBM, WHOLE, HBM, HBM], out_specs=[HBM, WHOLE],
+        scratch_shapes=buffers(field_shape, field_shape, narrow, tall, field_shape)
+        + [sems(2 + 4 * SPANS), sems(2 * SPANS)],
     )(field, cot, back.reshape(sent_shape), jnp.asarray(row_inv), turned(row_inv))
     arrived = across(sent, "pencil").reshape(height, wide)
     modes = modes_x * GROUP
-    dmixed, sent = call(
-        turn_kernel, [shaped((modes_x, wide)), shaped((height, wide))], "turn", 28,
-        in_specs=[WHOLE] * 6 + [ANY], out_specs=[WHOLE] * 2,
+    dmixed = column(turned(col_inv), arrived, "column_in_t")
+    all_dmixed = lax.all_gather(dmixed, "dp")
+    sent = call(
+        turn_kernel, shaped((height, wide)), "turn", 60,
+        in_specs=[WHOLE] * 5 + [HBM], out_specs=WHOLE,
         scratch_shapes=[
             pltpu.VMEM((modes, spectral_weight.shape[2]), BF16),
             pltpu.VMEM((modes, LANES), F32),
@@ -407,17 +456,21 @@
             sems(modes // (2 * LANES)),
         ],
     )(
-        turned(col_inv), arrived, order_in, order_out, turned(col_fwd), jnp.asarray(summed),
+        dmixed, order_in, order_out, turned(col_fwd), jnp.asarray(summed),
         gathered.reshape(modes, spectral_weight.shape[2]),
     )
     back = across(sent, "pencil").reshape(sent_shape)
+    own = spectral_weight.shape[0]
+    own_dmixed = lax.dynamic_slice_in_dim(all_dmixed, own * lax.axis_index("dp"), own, axis=1)
     grad_weight = call(
-        grad_kernel, shaped((GROUP, GROUP, channels, 2 * channels), F32), "weight_grad"
-    )(spectrum, across(dmixed, "dp"), order_in)
+        grad_kernel, shaped((GROUP, GROUP, channels, 2 * channels), F32), "weight_grad",
+        in_specs=[WHOLE] * 3 + [HBM], out_specs=WHOLE,
+    )(spectrum, own_dmixed.reshape(modes_x, wide), order_in, sent)
     grad_input = call(
-        row_out_kernel, shaped(field_shape), "row_out", 16,
-        in_specs=[WHOLE] * 3, out_specs=ANY,
-        scratch_shapes=buffers(field_shape) + [sems(chunks)],
+        row_out_kernel, shaped(field_shape), "row_out", 60,
+        in_specs=[HBM, WHOLE, HBM], out_specs=HBM,
+        scratch_shapes=buffers(field_shape, narrow, field_shape)
+        + [sems(chunks + 1), sems(chunks)],
     )(dpre, back, jnp.asarray(row_fwd_t))
     return (grad_input[None], grad_weight.reshape(spectral_weight.shape))
 

time: 176 us -> 181 us (1.028); the launches traced: 175 us -> 178 us
  Pallas kernels: 26.7 us -> 41.6 us
  local copies, waits for them, and re-layouts: 15 us -> 4.46 us
  blocking collectives: 90 us -> 80.7 us
  waiting for transfers between devices: 19.3 us -> 27.4 us
    all_gather x1 -> x2, waiting for transfers between devices: 0.01 us -> 22.1 us  [the longest x1 22 us: local(): all_dmixed = lax.all_gather(dmixed, 'dp')]
    all_to_all x2, waiting for transfers between devices: 18.6 us -> 5.32 us  [across(): return lax.all_to_all(values, axis, split_axis=0, concat_axis=0, tiled=True)]
    unnamed x32 -> x18, local copies, waits for them, and re-layouts: 13.3 us -> 1.88 us
    all_to_all x5 -> x4, blocking collectives: 90 us -> 80.7 us  [across(): return lax.all_to_all(values, axis, split_axis=0, concat_axis=0, tiled=True)]
    pallas_call x3, Pallas kernels: 14.1 us -> 22.5 us  [the longest x1 9.9 us: local(): call(row_in_kernel, [shaped(sent_shape), shaped(spectral_weight.shape)],...]
    pallas_call x1, Pallas kernels: 6.53 us -> 12.1 us  [local(): call(middle_kernel, [shaped(field_shape), shaped(sent_shape)], 'middle',...]
  transfers between devices with their start and end apart: 3 -> 4, of which waited for: 2 -> 2; matrix products, arithmetic and copies ran while one was open for 1% -> 1% of each run, Pallas kernels for 11% -> 15%
where the time goes in v1:
time: 181 us; the launch traced here: 178 us
  blocking collectives  80.7 us (45%)
  Pallas kernels  41.6 us (23%)
  waiting for transfers between devices  27.4 us (15%)
  between operations  14.2 us (8%)
  starting transfers between devices  9.89 us (5%)
  local copies, waits for them, and re-layouts  4.46 us (2%)
    all_to_all x4, blocking collectives, across(): return lax.all_to_all(values, axis, split_axis=0, concat_axis=0, tiled=True)  80.7 us
    all_gather x1, waiting for transfers between devices, local(): all_dmixed = lax.all_gather(dmixed, 'dp')  22 us
    pallas_call x1, Pallas kernels, local(): call(middle_kernel, [shaped(field_shape), shaped(sent_shape)], 'middle',...  12.1 us
    pallas_call x1, Pallas kernels, local(): call(row_in_kernel, [shaped(sent_shape), shaped(spectral_weight.shape)],...  9.9 us
    all_to_all x2, starting transfers between devices, across(): return lax.all_to_all(values, axis, split_axis=0, concat_axis=0, tiled=True)  9.81 us
    pallas_call x1, Pallas kernels, local(): call(turn_kernel, shaped((height, wide)), 'turn', 60, in_specs=[WHOLE] *...  7.03 us
    pallas_call x1, Pallas kernels, local(): call(row_out_kernel, shaped(field_shape), 'row_out', 60, in_specs=[HBM, W...  5.54 us
    all_to_all x2, waiting for transfers between devices, across(): return lax.all_to_all(values, axis, split_axis=0, concat_axis=0, tiled=True)  5.32 us
  transfers between devices with their start and end apart: 4, of which 2 were waited for; matrix products, arithmetic and copies ran while one was open for 1% of the time, Pallas kernels for 15%

profile of v1, /device:TPU:32, one launch (start us, length us, event | category | flops | bytes accessed | tf_op | source)
XLA Modules:
  0.0 178.3 jit_solution(7874975413704345097)
XLA Ops:
  7.2 0.0 copy-start.6
  7.2 0.0 copy-start.8
  7.2 0.0 all-gather.4.cloned.1.call-start
  7.2 0.0 copy-start.1
  7.2 0.0 copy-start.3
  7.3 9.9 %row_in.1 = (bf16[16,32,512]{2,1,0:T(8,128)(2,1)}, bf16[8,8,2048]{2,1,0:T(8,128)(2,1)}) custom-call(bf16[32,32,2048]{2,1,0:T(8,128)(2,1)} %bitcast.25, bf16[2048,256]{1,0:T(8,128)(2,1)} %constant.35.clone.table_hbm, bf16[8,8,2048]{2,1,0:T(8,128)(2,1)} %weight_hbm.1), custom_call_target="tpu_custom_call" | custom-call | tf_op jit(solution)/shard_map/row_in/pallas_call | solution.py:424
  17.2 0.0 copy-start.5
  17.2 0.0 all-gather.4.cloned.1.call-update
  17.2 27.6 %all_to_all.50 = bf16[16,32,512]{2,1,0:T(8,128)(2,1)S(1)} all-to-all(bf16[16,32,512]{2,1,0:T(8,128)(2,1)} %get-tuple-element.6), channel_id=1, replica_groups=mesh['dp'=16,'pencil'=16] {'pencil'}, dimensions={0} | all-to-all | bytes 1048576 | tf_op jit(solution)/shard_map/all_to_all | solution.py:389
  44.8 0.0 copy-done.6
  44.8 1.0 column_in.1
  45.7 4.6 %all-to-all-start.1 = ((bf16[16,8,512]{2,1,0:T(8,128)(2,1)}), bf16[16,8,512]{2,1,0:T(8,128)(2,1)S(1)}, u32[]{:S(2)}, u32[]{:S(2)}) async-start(bf16[16,8,512]{2,1,0:T(8,128)(2,1)} %bitcast.3), calls=%async_computation.1 | async-start | bytes 262144 | tf_op jit(solution)/shard_map/all_to_all | solution.py:389
  50.3 0.0 all-gather.6.cloned.1.call-start
  50.4 0.0 copy-done.8
  50.4 0.5 reshape.35.in_ref
  50.9 2.1 %weight_blocks.1.weight_ref = bf16[4,128,1024]{2,1,0:T(8,128)(2,1)S(1)} custom-call(bf16[8,8,32,64]{3,2,1,0:T(8,128)(2,1)S(1)} %reshape.35.in_ref), custom_call_target="tpu_custom_call" | custom-call | tf_op jit(solution)/shard_map/weight_blocks/pallas_call | solution.py:419
  53.0 5.3 %all-to-all-done.1 = bf16[16,8,512]{2,1,0:T(8,128)(2,1)S(1)} async-done(((bf16[16,8,512]{2,1,0:T(8,128)(2,1)}), bf16[16,8,512]{2,1,0:T(8,128)(2,1)S(1)}, u32[]{:S(2)}, u32[]{:S(2)}) %all-to-all-start.1) | async-done | bytes 131104 | tf_op jit(solution)/shard_map/all_to_all | solution.py:389
  58.3 0.0 copy-done.1
  58.3 0.0 copy-done.3
  58.3 0.8 mix.1
  59.1 9.3 %all_to_all.51 = bf16[16,8,512]{2,1,0:T(8,128)(2,1)S(1)} all-to-all(bf16[16,8,512]{2,1,0:T(8,128)(2,1)S(1)} %bitcast.24), channel_id=1, replica_groups=mesh['dp'=16,'pencil'=16] {'dp'}, dimensions={0} | all-to-all | bytes 262144 | tf_op jit(solution)/shard_map/all_to_all | solution.py:389
  68.4 0.0 copy-done.5
  68.4 0.3 column_out.1
  68.7 22.3 %all_to_all.52.back_ref = bf16[16,32,512]{2,1,0:T(8,128)(2,1)} all-to-all(bf16[16,32,512]{2,1,0:T(8,128)(2,1)S(1)} %bitcast.19), channel_id=1, replica_groups=mesh['dp'=16,'pencil'=16] {'pencil'}, dimensions={0} | all-to-all | bytes 1048576 | tf_op jit(solution)/shard_map/all_to_all | solution.py:389
  91.1 0.0 copy-start.4
  91.1 12.1 %middle.1 = (bf16[32,32,2048]{2,1,0:T(8,128)(2,1)}, bf16[16,32,512]{2,1,0:T(8,128)(2,1)}) custom-call(bf16[32,32,2048]{2,1,0:T(8,128)(2,1)} %bitcast.26, bf16[32,32,2048]{2,1,0:T(8,128)(2,1)} %bitcast.27, bf16[16,32,512]{2,1,0:T(8,128)(2,1)} %all_to_all.52.back_ref, bf16[256,2048]{1,0:T(8,128)(2,1)} %constant.38.clone.inv_hbm, ...), custom_call_target="tpu_custom_call" | custom-call | tf_op jit(solution)/shard_map/middle/pallas_call | solution.py:437
  103.2 21.4 %all_to_all.53 = bf16[16,32,512]{2,1,0:T(8,128)(2,1)S(1)} all-to-all(bf16[16,32,512]{2,1,0:T(8,128)(2,1)} %get-tuple-element.8), channel_id=1, replica_groups=mesh['dp'=16,'pencil'=16] {'pencil'}, dimensions={0} | all-to-all | bytes 1048576 | tf_op jit(solution)/shard_map/all_to_all | solution.py:389
  124.7 0.0 copy-done.4
  124.7 1.0 column_in_t.1.dmixed_ref
  125.6 0.0 copy-start.2
  125.6 0.0 all-gather.6.cloned.1.call-update
  125.6 0.0 all-gather.4.cloned.1.call-done
  125.7 7.0 %turn.1.after_hbm = bf16[512,512]{1,0:T(8,128)(2,1)} custom-call(bf16[128,512]{1,0:T(8,128)(2,1)} %column_in_t.1.dmixed_ref, bf16[512,512]{1,0:T(8,128)(2,1)} %constant.33.clone.order_ref, bf16[512,512]{1,0:T(8,128)(2,1)} %constant.34.clone.order_t_ref, bf16[1024,256]{1,0:T(8,128)(2,1)} %constant.41.clone.table_out_ref, ...), custom_call_target="tpu_custom_call" | custom-call | tf_op jit(solution)/shard_map/turn/pallas_call | solution.py:447
  132.7 5.2 %all-to-all-start.5 = ((bf16[16,32,512]{2,1,0:T(8,128)(2,1)}), bf16[16,32,512]{2,1,0:T(8,128)(2,1)S(1)}, u32[]{:S(2)}, u32[]{:S(2)}) async-start(bf16[16,32,512]{2,1,0:T(8,128)(2,1)} %bitcast.17), calls=%async_computation.5 | async-start | bytes 1048576 | tf_op jit(solution)/shard_map/all_to_all | solution.py:389
  137.9 22.0 %all-gather.6.cloned.1.call-done = bf16[2048,512]{1,0:T(8,128)(2,1)} async-done(((bf16[128,512]{1,0:T(8,128)(2,1)}), bf16[2048,512]{1,0:T(8,128)(2,1)}) %all-gather.6.cloned.1.call-update) | async-done | bytes 2097168 | tf_op jit(solution)/shard_map/all_gather | solution.py:446
  160.0 0.9 dynamic-slice_bitcast_fusion.dmixed_ref
  160.9 0.0 copy-done.2
  160.9 0.0 copy-start
  160.9 1.0 copy-done
  161.9 2.0 %weight_grad.1 = f32[8,8,32,64]{3,2,1,0:T(8,128)S(1)} custom-call(bf16[128,512]{1,0:T(8,128)(2,1)S(1)} %bitcast.22, bf16[128,512]{1,0:T(8,128)(2,1)S(1)} %dynamic-slice_bitcast_fusion.dmixed_ref, bf16[512,512]{1,0:T(8,128)(2,1)S(1)} %copy-done.2, bf16[512,512]{1,0:T(8,128)(2,1)S(1)} %copy-done), custom_call_target="tpu_custom_call" | custom-call | tf_op jit(solution)/shard_map/weight_grad/pallas_call | solution.py:465
  163.9 1.2 reshape.39
  165.1 0.0 all-to-all-done.5.back_ref
  165.1 0.0 copy-start.7
  165.1 0.8 copy-done.7
  165.9 5.5 %row_out.1 = bf16[32,32,2048]{2,1,0:T(8,128)(2,1)} custom-call(bf16[32,32,2048]{2,1,0:T(8,128)(2,1)} %get-tuple-element.7.dpre_hbm, bf16[16,32,512]{2,1,0:T(8,128)(2,1)} %copy-done.7, bf16[256,2048]{1,0:T(8,128)(2,1)} %constant.43.clone.table_hbm), custom_call_target="tpu_custom_call" | custom-call | tf_op jit(solution)/shard_map/row_out/pallas_call | solution.py:469
Async XLA Ops:
  7.2 37.6 %copy-start.6 = (bf16[256,1024]{1,0:T(8,128)(2,1)S(1)}, bf16[256,1024]{1,0:T(8,128)(2,1)}, u32[]{:S(2)}) copy-start(bf16[256,1024]{1,0:T(8,128)(2,1)} %constant.36.clone.table_ref) | copy-start | bytes 1572868
  7.2 43.2 %copy-start.8 = (bf16[8,8,2048]{2,1,0:T(8,128)(2,1)S(1)}, bf16[8,8,2048]{2,1,0:T(8,128)(2,1)}, u32[]{:S(2)}) copy-start(bf16[8,8,2048]{2,1,0:T(8,128)(2,1)} %weight_hbm.1) | copy-start | bytes 786436
  7.2 118.5 %all-gather.4.cloned.1.call-start = ((), (), s32[]{:S(2)}) async-start(), calls=%async_computation.6 | async-start | bytes 4456448 | tf_op jit(solution)/shard_map/all_gather | solution.py:429
  7.2 51.1 %copy-start.1 = (bf16[512,512]{1,0:T(8,128)(2,1)S(1)}, bf16[512,512]{1,0:T(8,128)(2,1)}, u32[]{:S(2)}) copy-start(bf16[512,512]{1,0:T(8,128)(2,1)} %constant.33.clone.order_ref) | copy-start | bytes 1572868
  7.2 51.1 %copy-start.3 = (bf16[512,512]{1,0:T(8,128)(2,1)S(1)}, bf16[512,512]{1,0:T(8,128)(2,1)}, u32[]{:S(2)}) copy-start(bf16[512,512]{1,0:T(8,128)(2,1)} %constant.34.clone.order_t_ref) | copy-start | bytes 1572868
  17.2 51.3 %copy-start.5 = (bf16[1024,256]{1,0:T(8,128)(2,1)S(1)}, bf16[1024,256]{1,0:T(8,128)(2,1)}, u32[]{:S(2)}) copy-start(bf16[1024,256]{1,0:T(8,128)(2,1)} %constant.37.clone.table_ref) | copy-start | bytes 1572868
  45.7 12.6 %all-to-all-start.1 = ((bf16[16,8,512]{2,1,0:T(8,128)(2,1)}), bf16[16,8,512]{2,1,0:T(8,128)(2,1)S(1)}, u32[]{:S(2)}, u32[]{:S(2)}) async-start(bf16[16,8,512]{2,1,0:T(8,128)(2,1)} %bitcast.3), calls=%async_computation.1 | async-start | bytes 262144 | tf_op jit(solution)/shard_map/all_to_all | solution.py:389
  50.3 109.6 %all-gather.6.cloned.1.call-start = ((), (), s32[]{:S(2)}) async-start(), calls=%async_computation.7 | async-start | bytes 2228224 | tf_op jit(solution)/shard_map/all_gather | solution.py:446
  91.1 33.6 %copy-start.4 = (bf16[256,1024]{1,0:T(8,128)(2,1)S(1)}, bf16[256,1024]{1,0:T(8,128)(2,1)}, u32[]{:S(2)}) copy-start(bf16[256,1024]{1,0:T(8,128)(2,1)} %constant.40.clone.table_ref) | copy-start | bytes 1572868
  125.6 35.3 %copy-start.2 = (bf16[512,512]{1,0:T(8,128)(2,1)S(1)}, bf16[512,512]{1,0:T(8,128)(2,1)}, u32[]{:S(2)}) copy-start(bf16[512,512]{1,0:T(8,128)(2,1)} %constant.33.clone.order_ref) | copy-start | bytes 1572868
  132.7 32.3 %all-to-all-start.5 = ((bf16[16,32,512]{2,1,0:T(8,128)(2,1)}), bf16[16,32,512]{2,1,0:T(8,128)(2,1)S(1)}, u32[]{:S(2)}, u32[]{:S(2)}) async-start(bf16[16,32,512]{2,1,0:T(8,128)(2,1)} %bitcast.17), calls=%async_computation.5 | async-start | bytes 1048576 | tf_op jit(solution)/shard_map/all_to_all | solution.py:389
  160.9 1.0 copy-start
  165.1 0.8 copy-start.7
Sparse Core Ops, SparseCore 0:
  17.3 47.3 all-gather.3
  125.8 34.1 all-gather.5

commit v2 on v0

--- a/solution.py
+++ b/solution.py
@@ -1,3 +1,4 @@
+import functools
 import math
 
 import jax
@@ -56,6 +57,10 @@
 
 def dot(a, b):
     return jnp.dot(a, b, preferred_element_type=F32)
+
+
+def dot_t(a, b):
+    return lax.dot_general(a, b, (((1,), (1,)), ((), ())), preferred_element_type=F32)
 
 
 def swap_groups(slabs):
@@ -142,44 +147,50 @@
         pack(jnp.concatenate(parts[h * per_half : (h + 1) * per_half], axis=0), out_ref, h)
 
 
-def middle_kernel(field_ref, cot_ref, back_ref, inv_ref, inv_t_ref, dpre_ref, out_ref):
+def middle_kernel(field_ref, cot_ref, back_ref, inv_ref, dpre_ref, out_ref):
     rows, columns = field_ref.shape[1:]
     tall = SLABS * rows
+    cuts = [slice(y, y + TILE) for y in range(0, columns, TILE)]
     for h in range(2):
         at = slice(h * SLABS, (h + 1) * SLABS)
         back = unpack(back_ref, h)
-        cuts = [slice(start, start + TILE) for start in range(0, columns, TILE)]
         total = jnp.zeros((tall, out_ref.shape[2] // 2), F32)
         branch = dot(back, inv_ref[:, cuts[0]])
         held = None
-        for n, cut in enumerate(cuts):
-            following = dot(back, inv_ref[:, cuts[n + 1]]) if n + 1 < len(cuts) else None
+        for m, cut in enumerate(cuts):
+            following = dot(back, inv_ref[:, cuts[m + 1]]) if m + 1 < len(cuts) else None
             pre = flat(field_ref[at, :, cut]).astype(F32) + branch
             dpre = (flat(cot_ref[at, :, cut]) * slope(pre)).astype(BF16)
             if held is not None:
-                total = total + dot(held, inv_t_ref[cuts[n - 1], :])
+                total = total + dot_t(held, inv_ref[:, cuts[m - 1]])
             dpre_ref[at, :, cut] = dpre.reshape(SLABS, rows, TILE)
             held, branch = dpre, following
-        total = total + dot(held, inv_t_ref[cuts[-1], :])
+        total = total + dot_t(held, inv_ref[:, cuts[-1]])
         pack(total, out_ref, h)
 
 
-def row_out_kernel(dpre_ref, back_ref, table_ref, out_hbm, out_ref, sems):
+def row_out_kernel(
+    dpre_hbm, back_ref, table_ref, out_hbm, dpre_ref, out_ref, sems, sent_sems
+):
     chunks = dpre_ref.shape[0] // CHUNK
     rows, columns = dpre_ref.shape[1:]
     per_half = SLABS // CHUNK
+    loads = [
+        load(dpre_hbm.at[chunk(i)], dpre_ref.at[chunk(i)], sems.at[i]) for i in range(chunks)
+    ]
     stores = []
     for h in range(2):
         back = unpack(back_ref, h)
         for n in range(per_half):
             i = h * per_half + n
+            loads[i].wait()
             left = back[n * CHUNK * rows : (n + 1) * CHUNK * rows]
             at = slice(i * CHUNK, (i + 1) * CHUNK)
             for start in range(0, columns, TILE):
                 cut = slice(start, start + TILE)
                 value = flat(dpre_ref[at, :, cut]).astype(F32) + dot(left, table_ref[:, cut])
                 out_ref[at, :, cut] = value.astype(BF16).reshape(CHUNK, rows, TILE)
-            stores.append(load(out_ref.at[chunk(i)], out_hbm.at[chunk(i)], sems.at[i]))
+            stores.append(load(out_ref.at[chunk(i)], out_hbm.at[chunk(i)], sent_sems.at[i]))
     for copy in stores:
         copy.wait()
 
@@ -206,54 +217,9 @@
             ]
 
 
-def column_kernel(table_ref, in_ref, out_ref):
+def column_kernel(table_ref, in_ref, *early_and_out):
+    out_ref = early_and_out[-1]
     lay_parts(dot(table_ref[...], stack_parts(in_ref[...])).astype(BF16), out_ref)
-
-
-def turn_kernel(
-    table_in_ref, in_ref, order_ref, order_t_ref, table_out_ref, sum_ref, weight_hbm,
-    dmixed_ref, out_ref,
-    weight_ref, same_ref, cross_ref, grad_ref, spec_ref, sems,
-):
-    rows = dmixed_ref.shape[0]
-    total = weight_ref.shape[0]
-    width = weight_ref.shape[1]
-    piece = 2 * LANES
-    loads = [
-        load(weight_hbm.at[pl.ds(at, piece)], weight_ref.at[pl.ds(at, piece)], sems.at[n])
-        for n, at in enumerate(range(0, total, piece))
-    ]
-    lay_parts(dot(table_in_ref[...], stack_parts(in_ref[...])).astype(BF16), dmixed_ref)
-    dmixed = dot(dmixed_ref[...], order_ref[...])
-    lane = lax.broadcasted_iota(jnp.int32, (rows, LANES), 1)
-    low = lane < LANES // 2
-    real = lane % (LANES // 2) < LANES // 4
-    for pair in range(GROUP // 2):
-        both = dmixed[:, pair * LANES : (pair + 1) * LANES]
-        other = pltpu.roll(both, LANES // 2, 1)
-        for i in range(2):
-            same = jnp.where(low, both, other) if i == 0 else jnp.where(low, other, both)
-            turned = pltpu.roll(same, LANES // 4, 1)
-            at = pl.ds(2 * pair + i, rows, stride=GROUP)
-            same_ref[at, :] = same
-            cross_ref[at, :] = jnp.where(real, turned, -turned)
-    for n, at in enumerate(range(0, total, piece)):
-        loads[n].wait()
-        cut = slice(at, at + piece)
-        weight = weight_ref[cut, :]
-        copies = width // LANES
-        same = jnp.concatenate([same_ref[cut, :].astype(BF16)] * copies, axis=1)
-        cross = jnp.concatenate([cross_ref[cut, :].astype(BF16)] * copies, axis=1)
-        re = dot(weight * same, sum_ref[...])
-        im = dot(weight * cross, sum_ref[...])
-        grad_ref[cut, :] = re + pltpu.roll(im, LANES // 4, 1)
-    for pair in range(GROUP // 2):
-        first = grad_ref[pl.ds(2 * pair, rows, stride=GROUP), :]
-        second = grad_ref[pl.ds(2 * pair + 1, rows, stride=GROUP), :]
-        both = jnp.where(low, first, pltpu.roll(second, LANES // 2, 1))
-        spec_ref[:, pair * LANES : (pair + 1) * LANES] = both.astype(BF16)
-    dspec = dot(spec_ref[...], order_t_ref[...]).astype(BF16)
-    lay_parts(dot(table_out_ref[...], stack_parts(dspec)).astype(BF16), out_ref)
 
 
 def weight_kernel(in_ref, out_ref):
@@ -278,7 +244,7 @@
     return lax.broadcasted_iota(jnp.int32, shape, axis) % GROUP
 
 
-def mix_kernel(in_ref, weight_ref, order_ref, order_t_ref, out_ref):
+def mix_kernel(transposed, in_ref, weight_ref, order_ref, order_t_ref, out_ref):
     values = dot(in_ref[...], order_ref[...]).astype(BF16)
     rows = values.shape[0]
     own = own_row((rows, LANES), 0)
@@ -288,14 +254,14 @@
         total = jnp.zeros((rows, LANES), F32)
         for j in range(GROUP):
             weight = weight_ref[pair, :, j * LANES : (j + 1) * LANES]
-            term = dot(left, weight)
+            term = dot_t(left, weight) if transposed else dot(left, weight)
             total = jnp.where(own == j, term, total)
         pieces.append(total.astype(BF16))
     mixed = jnp.concatenate(pieces, axis=1)
     out_ref[...] = dot(mixed, order_t_ref[...]).astype(BF16)
 
 
-def grad_kernel(spec_ref, dmixed_ref, order_ref, out_ref):
+def grad_kernel(spec_ref, dmixed_ref, order_ref, after_hbm, early_ref, out_ref):
     spec = dot(spec_ref[...], order_ref[...])
     dmixed = dot(dmixed_ref[...], order_ref[...]).astype(BF16)
     rows = spec.shape[0]
@@ -328,7 +294,7 @@
     )
 
 
-ANY = pl.BlockSpec(memory_space=pl.ANY)
+HBM = pl.BlockSpec(memory_space=pltpu.HBM)
 WHOLE = pl.BlockSpec(memory_space=pltpu.VMEM)
 
 
@@ -355,70 +321,57 @@
     row_fwd_t, row_inv = row_tables(columns, modes_y)
     col_fwd, col_inv = column_tables(height, modes_x)
     order = mode_order(channels)
-    lane = np.arange(spectral_weight.shape[2])
-    summed = (lane[:, None] // (2 * channels) == np.arange(LANES)[None, :]).astype(
-        ml_dtypes.bfloat16
-    )
     field = field_in[0]
     cot = cotangent[0]
     field_shape = field.shape
     sent_shape = (SLABS, rows_here, wide)
     tall = (columns, 2 * modes_y)
+    inv_table, row_table = jnp.asarray(row_inv), jnp.asarray(row_fwd_t)
 
     def turned(table):
         return jnp.asarray(np.ascontiguousarray(table.T))
 
-    def column(table, values, name):
-        return call(column_kernel, shaped((table.shape[0] // 2, wide)), name)(table, values)
-
-    gathered = lax.all_gather(spectral_weight, "dp", axis=0, tiled=True)
+    def column(table, values, name, *early):
+        return call(column_kernel, shaped((table.shape[0] // 2, wide)), name)(
+            table, values, *early
+        )
+
     weights = call(
         weight_kernel, shaped((GROUP // 2, LANES, GROUP * LANES)), "weight_blocks"
     )(spectral_weight.reshape(GROUP, GROUP, channels, 2 * channels))
     order_in, order_out = jnp.asarray(order), turned(order)
 
+    def mix(values, transposed, name):
+        kernel = functools.partial(mix_kernel, transposed)
+        mixed = call(kernel, shaped((modes_x, wide)), name)(values, weights, order_in, order_out)
+        return across(mixed, "dp")
+
     sent = call(
         row_in_kernel, shaped(sent_shape), "row_in", 60,
-        in_specs=[ANY] * 2, out_specs=WHOLE,
+        in_specs=[HBM] * 2, out_specs=WHOLE,
         scratch_shapes=buffers(field_shape, tall) + [sems(chunks + 1)],
     )(field, turned(row_fwd_t))
     arrived = across(sent, "pencil").reshape(height, wide)
     spectrum = across(column(jnp.asarray(col_fwd), arrived, "column_in"), "dp")
-    mixed = across(
-        call(mix_kernel, shaped((modes_x, wide)), "mix")(spectrum, weights, order_in, order_out),
-        "dp",
-    )
-    back = across(column(jnp.asarray(col_inv), mixed, "column_out"), "pencil")
+    mixed = mix(spectrum, False, "mix")
+    back = across(column(jnp.asarray(col_inv), mixed, "column_out", inv_table), "pencil")
     dpre, sent = call(
-        middle_kernel, [shaped(field_shape), shaped(sent_shape)], "middle", 16,
-        in_specs=[WHOLE] * 5, out_specs=[WHOLE] * 2,
-    )(field, cot, back.reshape(sent_shape), jnp.asarray(row_inv), turned(row_inv))
+        middle_kernel, [shaped(field_shape), shaped(sent_shape)], "middle", 24,
+        in_specs=[WHOLE] * 4, out_specs=[WHOLE] * 2,
+    )(field, cot, back.reshape(sent_shape), inv_table)
     arrived = across(sent, "pencil").reshape(height, wide)
-    modes = modes_x * GROUP
-    dmixed, sent = call(
-        turn_kernel, [shaped((modes_x, wide)), shaped((height, wide))], "turn", 28,
-        in_specs=[WHOLE] * 6 + [ANY], out_specs=[WHOLE] * 2,
-        scratch_shapes=[
-            pltpu.VMEM((modes, spectral_weight.shape[2]), BF16),
-            pltpu.VMEM((modes, LANES), F32),
-            pltpu.VMEM((modes, LANES), F32),
-            pltpu.VMEM((modes, LANES), F32),
-            pltpu.VMEM((modes_x, wide), BF16),
-            sems(modes // (2 * LANES)),
-        ],
-    )(
-        turned(col_inv), arrived, order_in, order_out, turned(col_fwd), jnp.asarray(summed),
-        gathered.reshape(modes, spectral_weight.shape[2]),
-    )
+    dmixed = across(column(turned(col_inv), arrived, "column_in_t"), "dp")
+    sent = column(turned(col_fwd), mix(dmixed, True, "mix_t"), "column_out_t")
     back = across(sent, "pencil").reshape(sent_shape)
     grad_weight = call(
-        grad_kernel, shaped((GROUP, GROUP, channels, 2 * channels), F32), "weight_grad"
-    )(spectrum, across(dmixed, "dp"), order_in)
+        grad_kernel, shaped((GROUP, GROUP, channels, 2 * channels), F32), "weight_grad",
+        in_specs=[WHOLE] * 3 + [HBM, WHOLE], out_specs=WHOLE,
+    )(spectrum, dmixed, order_in, sent, row_table)
     grad_input = call(
-        row_out_kernel, shaped(field_shape), "row_out", 16,
-        in_specs=[WHOLE] * 3, out_specs=ANY,
-        scratch_shapes=buffers(field_shape) + [sems(chunks)],
-    )(dpre, back, jnp.asarray(row_fwd_t))
+        row_out_kernel, shaped(field_shape), "row_out", 52,
+        in_specs=[HBM, WHOLE, WHOLE], out_specs=HBM,
+        scratch_shapes=buffers(field_shape, field_shape) + [sems(chunks)] * 2,
+    )(dpre, back, row_table)
     return (grad_input[None], grad_weight.reshape(spectral_weight.shape))
 
 

time: 176 us -> 160 us (0.909)
  between operations: 14.2 us -> 0.95 us
  blocking collectives: 90 us -> 99.5 us
  local copies, waits for them, and re-layouts: 15 us -> 6.15 us
  waiting for transfers between devices: 19.3 us -> 17.3 us
    all_to_all x5 -> x6, blocking collectives: 90 us -> 99.5 us  [across(): return lax.all_to_all(values, axis, split_axis=0, concat_axis=0, tiled=True)]
    unnamed x32 -> x26, local copies, waits for them, and re-layouts: 13.3 us -> 4.48 us
    pallas_call x4, Pallas kernels: 14.9 us -> 11.9 us  [the longest x1 5.81 us: local(): call(row_in_kernel, shaped(sent_shape), 'row_in', 60, in_specs=[HBM] * 2,...]
  transfers between devices with their start and end apart: 3 -> 2, of which waited for: 2 -> 2; matrix products, arithmetic and copies ran while one was open for 1% -> 1% of each run, Pallas kernels for 11% -> 3%
where the time goes in v2:
time: 160 us; the launch traced here: 159 us
  blocking collectives  99.5 us (62%)
  Pallas kernels  25.3 us (16%)
  waiting for transfers between devices  17.3 us (11%)
  starting transfers between devices  10.2 us (6%)
  local copies, waits for them, and re-layouts  6.15 us (4%)
    all_to_all x6, blocking collectives, across(): return lax.all_to_all(values, axis, split_axis=0, concat_axis=0, tiled=True)  99.5 us
    all_to_all x2, waiting for transfers between devices, across(): return lax.all_to_all(values, axis, split_axis=0, concat_axis=0, tiled=True)  17.3 us
    all_to_all x2, starting transfers between devices, across(): return lax.all_to_all(values, axis, split_axis=0, concat_axis=0, tiled=True)  10.2 us
    pallas_call x1, Pallas kernels, local(): call(middle_kernel, [shaped(field_shape), shaped(sent_shape)], 'middle',...  6.65 us
    pallas_call x1, Pallas kernels, local(): call(row_in_kernel, shaped(sent_shape), 'row_in', 60, in_specs=[HBM] * 2,...  5.81 us
    unnamed x26, local copies, waits for them, and re-layouts  4.48 us
    pallas_call x1, Pallas kernels, local(): call(row_out_kernel, shaped(field_shape), 'row_out', 52, in_specs=[HBM, W...  4.19 us
  transfers between devices with their start and end apart: 2, of which 2 were waited for; matrix products, arithmetic and copies ran while one was open for 1% of the time, Pallas kernels for 3%

profile of v2, /device:TPU:32, one launch (start us, length us, event | category | flops | bytes accessed | tf_op | source)
XLA Modules:
  0.0 159.3 jit_solution(12656403538379783502)
XLA Ops:
  0.6 0.0 copy-start.11
  0.6 0.0 copy-start.12
  0.7 0.0 copy-start.1
  0.7 5.8 %row_in.1 = bf16[16,32,512]{2,1,0:T(8,128)(2,1)} custom-call(bf16[32,32,2048]{2,1,0:T(8,128)(2,1)} %bitcast.17, bf16[2048,256]{1,0:T(8,128)(2,1)} %constant.22.clone.table_hbm), custom_call_target="tpu_custom_call" | custom-call | tf_op jit(solution)/shard_map/row_in/pallas_call | solution.py:349
  6.5 0.0 copy-start.3
  6.5 27.6 %all_to_all.72 = bf16[16,32,512]{2,1,0:T(8,128)(2,1)S(1)} all-to-all(bf16[16,32,512]{2,1,0:T(8,128)(2,1)} %row_in.1), channel_id=1, replica_groups=mesh['dp'=16,'pencil'=16] {'pencil'}, dimensions={0} | all-to-all | bytes 1048576 | tf_op jit(solution)/shard_map/all_to_all | solution.py:310
  34.0 0.0 copy-done.11
  34.1 1.0 column_in.1
  35.0 4.6 %all-to-all-start.1 = ((bf16[16,8,512]{2,1,0:T(8,128)(2,1)}), bf16[16,8,512]{2,1,0:T(8,128)(2,1)S(1)}, u32[]{:S(2)}, u32[]{:S(2)}) async-start(bf16[16,8,512]{2,1,0:T(8,128)(2,1)} %bitcast.3), calls=%async_computation.1 | async-start | bytes 262144 | tf_op jit(solution)/shard_map/all_to_all | solution.py:310
  39.6 0.0 copy-done.12
  39.6 0.5 reshape.33.in_ref
  40.2 2.1 %weight_blocks.1.weight_ref = bf16[4,128,1024]{2,1,0:T(8,128)(2,1)S(1)} custom-call(bf16[8,8,32,64]{3,2,1,0:T(8,128)(2,1)S(1)} %reshape.33.in_ref), custom_call_target="tpu_custom_call" | custom-call | tf_op jit(solution)/shard_map/weight_blocks/pallas_call | solution.py:339
  42.3 4.1 %all-to-all-done.1 = bf16[16,8,512]{2,1,0:T(8,128)(2,1)S(1)} async-done(((bf16[16,8,512]{2,1,0:T(8,128)(2,1)}), bf16[16,8,512]{2,1,0:T(8,128)(2,1)S(1)}, u32[]{:S(2)}, u32[]{:S(2)}) %all-to-all-start.1) | async-done | bytes 131104 | tf_op jit(solution)/shard_map/all_to_all | solution.py:310
  46.3 0.0 copy-done.1
  46.3 0.0 copy-start.6
  46.3 1.2 copy-done.6
  47.5 0.8 mix.1
  48.3 9.3 %all_to_all.73 = bf16[16,8,512]{2,1,0:T(8,128)(2,1)S(1)} all-to-all(bf16[16,8,512]{2,1,0:T(8,128)(2,1)S(1)} %bitcast.31), channel_id=1, replica_groups=mesh['dp'=16,'pencil'=16] {'dp'}, dimensions={0} | all-to-all | bytes 262144 | tf_op jit(solution)/shard_map/all_to_all | solution.py:310
  57.6 0.0 copy-done.3
  57.6 0.0 copy-start.8
  57.6 1.0 copy-done.8
  58.7 0.3 column_out.1
  59.0 22.1 %all_to_all.74.back_ref = bf16[16,32,512]{2,1,0:T(8,128)(2,1)S(1)} all-to-all(bf16[16,32,512]{2,1,0:T(8,128)(2,1)S(1)} %bitcast.20), channel_id=1, replica_groups=mesh['dp'=16,'pencil'=16] {'pencil'}, dimensions={0} | all-to-all | bytes 1048576 | tf_op jit(solution)/shard_map/all_to_all | solution.py:310
  81.1 0.0 copy-done
  81.1 0.0 copy-start.4
  81.1 2.2 %copy-done.4 = bf16[1,32,32,2048]{3,2,1,0:T(8,128)(2,1)S(1)} copy-done((bf16[1,32,32,2048]{3,2,1,0:T(8,128)(2,1)S(1)}, bf16[1,32,32,2048]{3,2,1,0:T(8,128)(2,1)}, u32[]{:S(2)}) %copy-start.4) | copy-done | bytes 4194328
  83.3 0.0 copy-start.10
  83.3 0.0 copy-start.7
  83.3 6.6 %middle.1 = (bf16[32,32,2048]{2,1,0:T(8,128)(2,1)S(1)}, bf16[16,32,512]{2,1,0:T(8,128)(2,1)S(1)}) custom-call(bf16[32,32,2048]{2,1,0:T(8,128)(2,1)S(1)} %bitcast.18, bf16[32,32,2048]{2,1,0:T(8,128)(2,1)S(1)} %bitcast.19, bf16[16,32,512]{2,1,0:T(8,128)(2,1)S(1)} %all_to_all.74.back_ref, bf16[256,2048]{1,0:T(8,128)(2,1)S(1)} %copy-done.3), custom_call_target="tpu_custom_call" | custom-call | tf_op jit(solution)/shard_map/middle/pallas_call | solution.py:358
  90.0 0.0 copy-start.5
  90.0 0.0 copy-start.9
  90.0 0.0 copy-start.2
  90.0 21.6 %all_to_all.75 = bf16[16,32,512]{2,1,0:T(8,128)(2,1)S(1)} all-to-all(bf16[16,32,512]{2,1,0:T(8,128)(2,1)S(1)} %get-tuple-element.5), channel_id=1, replica_groups=mesh['dp'=16,'pencil'=16] {'pencil'}, dimensions={0} | all-to-all | bytes 1048576 | tf_op jit(solution)/shard_map/all_to_all | solution.py:310
  111.6 0.0 copy-done.10
  111.6 0.3 column_in_t.1
  112.0 9.5 %all_to_all.76 = bf16[16,8,512]{2,1,0:T(8,128)(2,1)S(1)} all-to-all(bf16[16,8,512]{2,1,0:T(8,128)(2,1)S(1)} %bitcast.28), channel_id=1, replica_groups=mesh['dp'=16,'pencil'=16] {'dp'}, dimensions={0} | all-to-all | bytes 262144 | tf_op jit(solution)/shard_map/all_to_all | solution.py:310
  121.5 0.0 copy-done.7
  121.5 1.2 mix_t.1
  122.6 0.0 copy-done.5
  122.7 9.3 %all_to_all.77 = bf16[16,8,512]{2,1,0:T(8,128)(2,1)S(1)} all-to-all(bf16[16,8,512]{2,1,0:T(8,128)(2,1)S(1)} %bitcast.29), channel_id=1, replica_groups=mesh['dp'=16,'pencil'=16] {'dp'}, dimensions={0} | all-to-all | bytes 262144 | tf_op jit(solution)/shard_map/all_to_all | solution.py:310
  132.0 0.0 copy-done.9
  132.0 1.1 column_out_t.1.after_hbm
  133.1 5.6 %all-to-all-start.7 = ((bf16[16,32,512]{2,1,0:T(8,128)(2,1)}), bf16[16,32,512]{2,1,0:T(8,128)(2,1)S(1)}, u32[]{:S(2)}, u32[]{:S(2)}) async-start(bf16[16,32,512]{2,1,0:T(8,128)(2,1)} %bitcast.13), calls=%async_computation.7 | async-start | bytes 1048576 | tf_op jit(solution)/shard_map/all_to_all | solution.py:310
  138.6 0.0 copy-done.2
  138.6 2.0 %weight_grad.1 = f32[8,8,32,64]{3,2,1,0:T(8,128)S(1)} custom-call(bf16[128,512]{1,0:T(8,128)(2,1)S(1)} %bitcast.24, bf16[128,512]{1,0:T(8,128)(2,1)S(1)} %bitcast.26, bf16[512,512]{1,0:T(8,128)(2,1)S(1)} %copy-done.1, bf16[512,512]{1,0:T(8,128)(2,1)} %column_out_t.1.after_hbm, bf16[256,2048]{1,0:T(8,128)(2,1)S(1)} %copy-done.2), custom_call_target="tpu_custom_call" | custom-call | tf_op jit(solution)/shard_map/weight_grad/pallas_call | solution.py:366
  140.6 1.2 reshape.35
  141.8 13.2 %all-to-all-done.7.back_ref = bf16[16,32,512]{2,1,0:T(8,128)(2,1)S(1)} async-done(((bf16[16,32,512]{2,1,0:T(8,128)(2,1)}), bf16[16,32,512]{2,1,0:T(8,128)(2,1)S(1)}, u32[]{:S(2)}, u32[]{:S(2)}) %all-to-all-start.7) | async-done | bytes 524320 | tf_op jit(solution)/shard_map/all_to_all | solution.py:310
  155.0 4.2 %row_out.1 = bf16[32,32,2048]{2,1,0:T(8,128)(2,1)} custom-call(bf16[32,32,2048]{2,1,0:T(8,128)(2,1)} %copy-done.5, bf16[16,32,512]{2,1,0:T(8,128)(2,1)S(1)} %all-to-all-done.7.back_ref, bf16[256,2048]{1,0:T(8,128)(2,1)S(1)} %copy-done.2), custom_call_target="tpu_custom_call" | custom-call | tf_op jit(solution)/shard_map/row_out/pallas_call | solution.py:370
  (1 shorter events, 0.0 us)
Async XLA Ops:
  0.6 33.4 %copy-start.11 = (bf16[256,1024]{1,0:T(8,128)(2,1)S(1)}, bf16[256,1024]{1,0:T(8,128)(2,1)}, u32[]{:S(2)}) copy-start(bf16[256,1024]{1,0:T(8,128)(2,1)} %constant.23.clone.table_ref) | copy-start | bytes 1572868
  0.6 39.0 %copy-start.12 = (bf16[8,8,2048]{2,1,0:T(8,128)(2,1)S(1)}, bf16[8,8,2048]{2,1,0:T(8,128)(2,1)}, u32[]{:S(2)}) copy-start(bf16[8,8,2048]{2,1,0:T(8,128)(2,1)} %param.14) | copy-start | bytes 786436
  0.7 45.7 %copy-start.1 = (bf16[512,512]{1,0:T(8,128)(2,1)S(1)}, bf16[512,512]{1,0:T(8,128)(2,1)}, u32[]{:S(2)}) copy-start(bf16[512,512]{1,0:T(8,128)(2,1)} %constant.20.clone.order_ref) | copy-start | bytes 1572868
  6.5 51.2 %copy-start.3 = (bf16[256,2048]{1,0:T(8,128)(2,1)S(1)}, bf16[256,2048]{1,0:T(8,128)(2,1)}, u32[]{:S(2)}) copy-start(bf16[256,2048]{1,0:T(8,128)(2,1)} %constant.18.clone.early_and_out_0_.inv_ref) | copy-start | bytes 3145732
  35.0 11.3 %all-to-all-start.1 = ((bf16[16,8,512]{2,1,0:T(8,128)(2,1)}), bf16[16,8,512]{2,1,0:T(8,128)(2,1)S(1)}, u32[]{:S(2)}, u32[]{:S(2)}) async-start(bf16[16,8,512]{2,1,0:T(8,128)(2,1)} %bitcast.3), calls=%async_computation.1 | async-start | bytes 262144 | tf_op jit(solution)/shard_map/all_to_all | solution.py:310
  46.3 34.8 %copy-start = (bf16[1,32,32,2048]{3,2,1,0:T(8,128)(2,1)S(1)}, bf16[1,32,32,2048]{3,2,1,0:T(8,128)(2,1)}, u32[]{:S(2)}) copy-start(bf16[1,32,32,2048]{3,2,1,0:T(8,128)(2,1)} %param.12) | copy-start | bytes 12582916
  46.3 1.2 copy-start.6
  57.6 1.0 copy-start.8
  81.1 2.2 %copy-start.4 = (bf16[1,32,32,2048]{3,2,1,0:T(8,128)(2,1)S(1)}, bf16[1,32,32,2048]{3,2,1,0:T(8,128)(2,1)}, u32[]{:S(2)}) copy-start(bf16[1,32,32,2048]{3,2,1,0:T(8,128)(2,1)} %param.13) | copy-start | bytes 12582916
  83.3 28.3 %copy-start.10 = (bf16[256,1024]{1,0:T(8,128)(2,1)S(1)}, bf16[256,1024]{1,0:T(8,128)(2,1)}, u32[]{:S(2)}) copy-start(bf16[256,1024]{1,0:T(8,128)(2,1)} %constant.25.clone.table_ref) | copy-start | bytes 1572868
  83.3 38.2 %copy-start.7 = (bf16[512,512]{1,0:T(8,128)(2,1)S(1)}, bf16[512,512]{1,0:T(8,128)(2,1)}, u32[]{:S(2)}) copy-start(bf16[512,512]{1,0:T(8,128)(2,1)} %constant.21.clone.order_t_ref) | copy-start | bytes 1572868
  90.0 32.7 %copy-start.5 = (bf16[32,32,2048]{2,1,0:T(8,128)(2,1)}, bf16[32,32,2048]{2,1,0:T(8,128)(2,1)S(1)}, u32[]{:S(2)}) copy-start(bf16[32,32,2048]{2,1,0:T(8,128)(2,1)S(1)} %get-tuple-element.4.dpre_hbm) | copy-start | bytes 12582916
  90.0 42.0 %copy-start.9 = (bf16[1024,256]{1,0:T(8,128)(2,1)S(1)}, bf16[1024,256]{1,0:T(8,128)(2,1)}, u32[]{:S(2)}) copy-start(bf16[1024,256]{1,0:T(8,128)(2,1)} %constant.26.clone.table_ref) | copy-start | bytes 1572868
  90.0 48.6 %copy-start.2 = (bf16[256,2048]{1,0:T(8,128)(2,1)S(1)}, bf16[256,2048]{1,0:T(8,128)(2,1)}, u32[]{:S(2)}) copy-start(bf16[256,2048]{1,0:T(8,128)(2,1)} %constant.19.clone.table_ref.early_ref) | copy-start | bytes 3145732
  133.1 21.9 %all-to-all-start.7 = ((bf16[16,32,512]{2,1,0:T(8,128)(2,1)}), bf16[16,32,512]{2,1,0:T(8,128)(2,1)S(1)}, u32[]{:S(2)}, u32[]{:S(2)}) async-start(bf16[16,32,512]{2,1,0:T(8,128)(2,1)} %bitcast.13), calls=%async_computation.7 | async-start | bytes 1048576 | tf_op jit(solution)/shard_map/all_to_all | solution.py:310

commit v3 on v2

--- a/solution.py
+++ b/solution.py
@@ -147,15 +147,20 @@
         pack(jnp.concatenate(parts[h * per_half : (h + 1) * per_half], axis=0), out_ref, h)
 
 
-def middle_kernel(field_ref, cot_ref, back_ref, inv_ref, dpre_ref, out_ref):
+def middle_kernel(
+    field_ref, cot_hbm, back_ref, inv_ref, dpre_ref, out_ref, cot_ref, sems
+):
     rows, columns = field_ref.shape[1:]
     tall = SLABS * rows
+    halves = [pl.ds(h * SLABS, SLABS) for h in range(2)]
+    loads = [load(cot_hbm.at[at], cot_ref.at[at], sems.at[h]) for h, at in enumerate(halves)]
     cuts = [slice(y, y + TILE) for y in range(0, columns, TILE)]
     for h in range(2):
         at = slice(h * SLABS, (h + 1) * SLABS)
         back = unpack(back_ref, h)
         total = jnp.zeros((tall, out_ref.shape[2] // 2), F32)
         branch = dot(back, inv_ref[:, cuts[0]])
+        loads[h].wait()
         held = None
         for m, cut in enumerate(cuts):
             following = dot(back, inv_ref[:, cuts[m + 1]]) if m + 1 < len(cuts) else None
@@ -222,7 +227,8 @@
     lay_parts(dot(table_ref[...], stack_parts(in_ref[...])).astype(BF16), out_ref)
 
 
-def weight_kernel(in_ref, out_ref):
+def weight_kernel(in_ref, *early_and_out):
+    out_ref = early_and_out[-1]
     modes, channels = in_ref.shape[0], in_ref.shape[2]
     zero = jnp.zeros((2 * channels, 2 * channels), F32)
     for j in range(modes):
@@ -336,10 +342,14 @@
             table, values, *early
         )
 
+    order_in, order_out = jnp.asarray(order), turned(order)
+    fwd_table, col_table = jnp.asarray(col_fwd), jnp.asarray(col_inv)
     weights = call(
         weight_kernel, shaped((GROUP // 2, LANES, GROUP * LANES)), "weight_blocks"
-    )(spectral_weight.reshape(GROUP, GROUP, channels, 2 * channels))
-    order_in, order_out = jnp.asarray(order), turned(order)
+    )(
+        spectral_weight.reshape(GROUP, GROUP, channels, 2 * channels),
+        order_in, order_out, col_table,
+    )
 
     def mix(values, transposed, name):
         kernel = functools.partial(mix_kernel, transposed)
@@ -352,12 +362,14 @@
         scratch_shapes=buffers(field_shape, tall) + [sems(chunks + 1)],
     )(field, turned(row_fwd_t))
     arrived = across(sent, "pencil").reshape(height, wide)
-    spectrum = across(column(jnp.asarray(col_fwd), arrived, "column_in"), "dp")
+    modes = column(fwd_table, arrived, "column_in", weights)
+    spectrum = across(modes, "dp")
     mixed = mix(spectrum, False, "mix")
-    back = across(column(jnp.asarray(col_inv), mixed, "column_out", inv_table), "pencil")
+    back = across(column(col_table, mixed, "column_out", inv_table), "pencil")
     dpre, sent = call(
-        middle_kernel, [shaped(field_shape), shaped(sent_shape)], "middle", 24,
-        in_specs=[WHOLE] * 4, out_specs=[WHOLE] * 2,
+        middle_kernel, [shaped(field_shape), shaped(sent_shape)], "middle", 40,
+        in_specs=[WHOLE, HBM, WHOLE, WHOLE], out_specs=[WHOLE] * 2,
+        scratch_shapes=buffers(field_shape) + [sems(2)],
     )(field, cot, back.reshape(sent_shape), inv_table)
     arrived = across(sent, "pencil").reshape(height, wide)
     dmixed = across(column(turned(col_inv), arrived, "column_in_t"), "dp")

time: 160 us -> 159 us (level)
  blocking collectives: 99.5 us -> 82.9 us
  waiting for transfers between devices: 17.3 us -> 24.2 us
  starting transfers between devices: 10.2 us -> 16.6 us
  Pallas kernels: 25.3 us -> 27.6 us
    all_to_all x6, blocking collectives: 99.5 us -> 82.9 us  [across(): return lax.all_to_all(values, axis, split_axis=0, concat_axis=0, tiled=True)]
    all_to_all x2, waiting for transfers between devices: 17.3 us -> 24.2 us  [across(): return lax.all_to_all(values, axis, split_axis=0, concat_axis=0, tiled=True)]
    all_to_all x2, starting transfers between devices: 10.2 us -> 16.6 us  [across(): return lax.all_to_all(values, axis, split_axis=0, concat_axis=0, tiled=True)]
    pallas_call x1, Pallas kernels: 6.65 us -> 8.48 us  [local(): call(middle_kernel, [shaped(field_shape), shaped(sent_shape)], 'middle',...]
  transfers between devices with their start and end apart: 2 -> 2, of which waited for: 2 -> 2; matrix products, arithmetic and copies ran while one was open for 1% -> 2% of each run, Pallas kernels for 3% -> 3%
where the time goes in v3:
time: 159 us; the launch traced here: 158 us
  blocking collectives  82.9 us (52%)
  Pallas kernels  27.6 us (17%)
  waiting for transfers between devices  24.2 us (15%)
  starting transfers between devices  16.6 us (10%)
  local copies, waits for them, and re-layouts  5.71 us (4%)
    all_to_all x6, blocking collectives, across(): return lax.all_to_all(values, axis, split_axis=0, concat_axis=0, tiled=True)  82.9 us
    all_to_all x2, waiting for transfers between devices, across(): return lax.all_to_all(values, axis, split_axis=0, concat_axis=0, tiled=True)  24.2 us
    all_to_all x2, starting transfers between devices, across(): return lax.all_to_all(values, axis, split_axis=0, concat_axis=0, tiled=True)  16.6 us
    pallas_call x1, Pallas kernels, local(): call(middle_kernel, [shaped(field_shape), shaped(sent_shape)], 'middle',...  8.48 us
    pallas_call x1, Pallas kernels, local(): call(row_in_kernel, shaped(sent_shape), 'row_in', 60, in_specs=[HBM] * 2,...  5.81 us
    pallas_call x1, Pallas kernels, local(): call(row_out_kernel, shaped(field_shape), 'row_out', 52, in_specs=[HBM, W...  4.18 us
    unnamed x26, local copies, waits for them, and re-layouts  3.23 us
    pallas_call x4, Pallas kernels, column(): call(column_kernel, shaped((table.shape[0] // 2, wide)), name)  3.18 us
  transfers between devices with their start and end apart: 2, of which 2 were waited for; matrix products, arithmetic and copies ran while one was open for 2% of the time, Pallas kernels for 3%

profile of v3, /device:TPU:32, one launch (start us, length us, event | category | flops | bytes accessed | tf_op | source)
XLA Modules:
  0.0 158.0 jit_solution(2092436028620378315)
XLA Ops:
  0.6 0.0 copy-start.1
  0.6 0.0 copy-start.2
  0.7 0.0 copy-start.12
  0.7 5.8 %row_in.1 = bf16[16,32,512]{2,1,0:T(8,128)(2,1)} custom-call(bf16[32,32,2048]{2,1,0:T(8,128)(2,1)} %bitcast.17, bf16[2048,256]{1,0:T(8,128)(2,1)} %constant.24.clone.table_hbm), custom_call_target="tpu_custom_call" | custom-call | tf_op jit(solution)/shard_map/row_in/pallas_call | solution.py:359
  6.5 11.1 %all-to-all-start = ((bf16[16,32,512]{2,1,0:T(8,128)(2,1)}), bf16[16,32,512]{2,1,0:T(8,128)(2,1)}, u32[]{:S(2)}, u32[]{:S(2)}) async-start(bf16[16,32,512]{2,1,0:T(8,128)(2,1)} %row_in.1), calls=%async_computation | async-start | bytes 1048576 | tf_op jit(solution)/shard_map/all_to_all | solution.py:316
  17.5 0.0 copy-done.12
  17.5 1.3 reshape.33.in_ref
  18.9 0.0 copy-done.1
  18.9 0.0 copy-done.2
  18.9 1.0 copy-done.6
  19.9 0.0 copy-start.8
  19.9 1.0 copy-done.8
  21.0 0.0 copy-start.4
  21.0 2.1 %weight_blocks.1.early_and_out_0_.weight_ref = bf16[4,128,1024]{2,1,0:T(8,128)(2,1)S(1)} custom-call(bf16[8,8,32,64]{3,2,1,0:T(8,128)(2,1)S(1)} %copy-done.8, bf16[512,512]{1,0:T(8,128)(2,1)S(1)} %copy-done.1, bf16[512,512]{1,0:T(8,128)(2,1)S(1)} %copy-done.2, bf16[1024,256]{1,0:T(8,128)(2,1)S(1)} %copy-done.6), custom_call_target="tpu_custom_call" | custom-call | tf_op jit(solution)/shard_map/weight_blocks/pallas_call | solution.py:347
  23.1 11.0 %all-to-all-done = bf16[16,32,512]{2,1,0:T(8,128)(2,1)} async-done(((bf16[16,32,512]{2,1,0:T(8,128)(2,1)}), bf16[16,32,512]{2,1,0:T(8,128)(2,1)}, u32[]{:S(2)}, u32[]{:S(2)}) %all-to-all-start) | async-done | bytes 524320 | tf_op jit(solution)/shard_map/all_to_all | solution.py:316
  34.0 0.0 copy-start.7
  34.0 0.0 copy-start.9
  34.0 1.1 copy-done.9
  35.1 0.0 copy-start
  35.1 1.5 column_in.1
  36.6 11.1 %all_to_all.72 = bf16[16,8,512]{2,1,0:T(8,128)(2,1)S(1)} all-to-all(bf16[16,8,512]{2,1,0:T(8,128)(2,1)S(1)} %bitcast.25), channel_id=1, replica_groups=mesh['dp'=16,'pencil'=16] {'dp'}, dimensions={0} | all-to-all | bytes 262144 | tf_op jit(solution)/shard_map/all_to_all | solution.py:316
  47.7 0.8 mix.1
  48.5 9.3 %all_to_all.73 = bf16[16,8,512]{2,1,0:T(8,128)(2,1)S(1)} all-to-all(bf16[16,8,512]{2,1,0:T(8,128)(2,1)S(1)} %bitcast.30), channel_id=1, replica_groups=mesh['dp'=16,'pencil'=16] {'dp'}, dimensions={0} | all-to-all | bytes 262144 | tf_op jit(solution)/shard_map/all_to_all | solution.py:316
  57.8 0.0 copy-done.4
  57.8 0.0 copy-done.7
  57.8 0.3 column_out.1
  58.1 22.1 %all_to_all.74.back_ref = bf16[16,32,512]{2,1,0:T(8,128)(2,1)S(1)} all-to-all(bf16[16,32,512]{2,1,0:T(8,128)(2,1)S(1)} %bitcast.19), channel_id=1, replica_groups=mesh['dp'=16,'pencil'=16] {'pencil'}, dimensions={0} | all-to-all | bytes 1048576 | tf_op jit(solution)/shard_map/all_to_all | solution.py:316
  80.2 0.0 copy-done
  80.3 0.0 copy-start.11
  80.3 8.5 %middle.1 = (bf16[32,32,2048]{2,1,0:T(8,128)(2,1)S(1)}, bf16[16,32,512]{2,1,0:T(8,128)(2,1)S(1)}) custom-call(bf16[32,32,2048]{2,1,0:T(8,128)(2,1)S(1)} %bitcast.18, bf16[32,32,2048]{2,1,0:T(8,128)(2,1)} %bitcast.31, bf16[16,32,512]{2,1,0:T(8,128)(2,1)S(1)} %all_to_all.74.back_ref, bf16[256,2048]{1,0:T(8,128)(2,1)S(1)} %copy-done.4), custom_call_target="tpu_custom_call" | custom-call | tf_op jit(solution)/shard_map/middle/pallas_call | solution.py:369
  88.7 0.0 copy-start.5
  88.7 0.0 copy-start.10
  88.8 0.0 copy-start.3
  88.8 21.4 %all_to_all.75 = bf16[16,32,512]{2,1,0:T(8,128)(2,1)S(1)} all-to-all(bf16[16,32,512]{2,1,0:T(8,128)(2,1)S(1)} %get-tuple-element.5), channel_id=1, replica_groups=mesh['dp'=16,'pencil'=16] {'pencil'}, dimensions={0} | all-to-all | bytes 1048576 | tf_op jit(solution)/shard_map/all_to_all | solution.py:316
  110.2 0.0 copy-done.11
  110.2 0.3 column_in_t.1
  110.5 9.6 %all_to_all.76 = bf16[16,8,512]{2,1,0:T(8,128)(2,1)S(1)} all-to-all(bf16[16,8,512]{2,1,0:T(8,128)(2,1)S(1)} %bitcast.27), channel_id=1, replica_groups=mesh['dp'=16,'pencil'=16] {'dp'}, dimensions={0} | all-to-all | bytes 262144 | tf_op jit(solution)/shard_map/all_to_all | solution.py:316
  120.1 1.2 mix_t.1
  121.2 0.0 copy-done.5
  121.3 9.3 %all_to_all.77 = bf16[16,8,512]{2,1,0:T(8,128)(2,1)S(1)} all-to-all(bf16[16,8,512]{2,1,0:T(8,128)(2,1)S(1)} %bitcast.28), channel_id=1, replica_groups=mesh['dp'=16,'pencil'=16] {'dp'}, dimensions={0} | all-to-all | bytes 262144 | tf_op jit(solution)/shard_map/all_to_all | solution.py:316
  130.6 0.0 copy-done.10
  130.6 1.1 column_out_t.1.after_hbm
  131.7 5.6 %all-to-all-start.7 = ((bf16[16,32,512]{2,1,0:T(8,128)(2,1)}), bf16[16,32,512]{2,1,0:T(8,128)(2,1)S(1)}, u32[]{:S(2)}, u32[]{:S(2)}) async-start(bf16[16,32,512]{2,1,0:T(8,128)(2,1)} %bitcast.13), calls=%async_computation.7 | async-start | bytes 1048576 | tf_op jit(solution)/shard_map/all_to_all | solution.py:316
  137.2 0.0 copy-done.3
  137.2 2.0 %weight_grad.1 = f32[8,8,32,64]{3,2,1,0:T(8,128)S(1)} custom-call(bf16[128,512]{1,0:T(8,128)(2,1)S(1)} %bitcast.22, bf16[128,512]{1,0:T(8,128)(2,1)S(1)} %bitcast.24, bf16[512,512]{1,0:T(8,128)(2,1)S(1)} %copy-done.1, bf16[512,512]{1,0:T(8,128)(2,1)} %column_out_t.1.after_hbm, bf16[256,2048]{1,0:T(8,128)(2,1)S(1)} %copy-done.3), custom_call_target="tpu_custom_call" | custom-call | tf_op jit(solution)/shard_map/weight_grad/pallas_call | solution.py:378
  139.2 1.2 reshape.35
  140.4 13.2 %all-to-all-done.7.back_ref = bf16[16,32,512]{2,1,0:T(8,128)(2,1)S(1)} async-done(((bf16[16,32,512]{2,1,0:T(8,128)(2,1)}), bf16[16,32,512]{2,1,0:T(8,128)(2,1)S(1)}, u32[]{:S(2)}, u32[]{:S(2)}) %all-to-all-start.7) | async-done | bytes 524320 | tf_op jit(solution)/shard_map/all_to_all | solution.py:316
  153.6 4.2 %row_out.1 = bf16[32,32,2048]{2,1,0:T(8,128)(2,1)} custom-call(bf16[32,32,2048]{2,1,0:T(8,128)(2,1)} %copy-done.5, bf16[16,32,512]{2,1,0:T(8,128)(2,1)S(1)} %all-to-all-done.7.back_ref, bf16[256,2048]{1,0:T(8,128)(2,1)S(1)} %copy-done.3), custom_call_target="tpu_custom_call" | custom-call | tf_op jit(solution)/shard_map/row_out/pallas_call | solution.py:382
  (1 shorter events, 0.0 us)
Async XLA Ops:
  0.6 18.2 %copy-start.1 = (bf16[512,512]{1,0:T(8,128)(2,1)S(1)}, bf16[512,512]{1,0:T(8,128)(2,1)}, u32[]{:S(2)}) copy-start(bf16[512,512]{1,0:T(8,128)(2,1)} %constant.20.clone.early_and_out_0_.order_ref) | copy-start | bytes 1572868
  0.6 18.2 %copy-start.2 = (bf16[512,512]{1,0:T(8,128)(2,1)S(1)}, bf16[512,512]{1,0:T(8,128)(2,1)}, u32[]{:S(2)}) copy-start(bf16[512,512]{1,0:T(8,128)(2,1)} %constant.21.clone.early_and_out_1_.order_t_ref) | copy-start | bytes 1572868
  0.7 16.9 %copy-start.12 = (bf16[8,8,2048]{2,1,0:T(8,128)(2,1)S(1)}, bf16[8,8,2048]{2,1,0:T(8,128)(2,1)}, u32[]{:S(2)}) copy-start(bf16[8,8,2048]{2,1,0:T(8,128)(2,1)} %param.14) | copy-start | bytes 786436
  6.5 27.5 %all-to-all-start = ((bf16[16,32,512]{2,1,0:T(8,128)(2,1)}), bf16[16,32,512]{2,1,0:T(8,128)(2,1)}, u32[]{:S(2)}, u32[]{:S(2)}) async-start(bf16[16,32,512]{2,1,0:T(8,128)(2,1)} %row_in.1), calls=%async_computation | async-start | bytes 1048576 | tf_op jit(solution)/shard_map/all_to_all | solution.py:316
  18.9 1.0 copy-start.6
  19.9 1.0 copy-start.8
  21.0 36.9 %copy-start.4 = (bf16[256,2048]{1,0:T(8,128)(2,1)S(1)}, bf16[256,2048]{1,0:T(8,128)(2,1)}, u32[]{:S(2)}) copy-start(bf16[256,2048]{1,0:T(8,128)(2,1)} %constant.18.clone.early_and_out_0_.inv_ref) | copy-start | bytes 3145732
  34.0 23.8 %copy-start.7 = (bf16[1024,256]{1,0:T(8,128)(2,1)S(1)}, bf16[1024,256]{1,0:T(8,128)(2,1)}, u32[]{:S(2)}) copy-start(bf16[1024,256]{1,0:T(8,128)(2,1)} %constant.23.clone.early_and_out_2_.table_ref) | copy-start | bytes 1572868
  34.0 1.1 copy-start.9
  35.1 45.1 %copy-start = (bf16[1,32,32,2048]{3,2,1,0:T(8,128)(2,1)S(1)}, bf16[1,32,32,2048]{3,2,1,0:T(8,128)(2,1)}, u32[]{:S(2)}) copy-start(bf16[1,32,32,2048]{3,2,1,0:T(8,128)(2,1)} %param.12) | copy-start | bytes 12582916
  80.3 30.0 %copy-start.11 = (bf16[256,1024]{1,0:T(8,128)(2,1)S(1)}, bf16[256,1024]{1,0:T(8,128)(2,1)}, u32[]{:S(2)}) copy-start(bf16[256,1024]{1,0:T(8,128)(2,1)} %constant.25.clone.table_ref) | copy-start | bytes 1572868
  88.7 32.5 %copy-start.5 = (bf16[32,32,2048]{2,1,0:T(8,128)(2,1)}, bf16[32,32,2048]{2,1,0:T(8,128)(2,1)S(1)}, u32[]{:S(2)}) copy-start(bf16[32,32,2048]{2,1,0:T(8,128)(2,1)S(1)} %get-tuple-element.4.dpre_hbm) | copy-start | bytes 12582916
  88.7 41.8 %copy-start.10 = (bf16[1024,256]{1,0:T(8,128)(2,1)S(1)}, bf16[1024,256]{1,0:T(8,128)(2,1)}, u32[]{:S(2)}) copy-start(bf16[1024,256]{1,0:T(8,128)(2,1)} %constant.26.clone.table_ref) | copy-start | bytes 1572868
  88.8 48.5 %copy-start.3 = (bf16[256,2048]{1,0:T(8,128)(2,1)S(1)}, bf16[256,2048]{1,0:T(8,128)(2,1)}, u32[]{:S(2)}) copy-start(bf16[256,2048]{1,0:T(8,128)(2,1)} %constant.19.clone.table_ref.early_ref) | copy-start | bytes 3145732
  131.7 21.9 %all-to-all-start.7 = ((bf16[16,32,512]{2,1,0:T(8,128)(2,1)}), bf16[16,32,512]{2,1,0:T(8,128)(2,1)S(1)}, u32[]{:S(2)}, u32[]{:S(2)}) async-start(bf16[16,32,512]{2,1,0:T(8,128)(2,1)} %bitcast.13), calls=%async_computation.7 | async-start | bytes 1048576 | tf_op jit(solution)/shard_map/all_to_all | solution.py:316

commit v4 on v3

--- a/solution.py
+++ b/solution.py
@@ -132,19 +132,18 @@
 
 
 def row_in_kernel(field_hbm, table_hbm, out_ref, field_ref, table_ref, sems):
-    chunks = field_ref.shape[0] // CHUNK
-    first = load(table_hbm, table_ref, sems.at[chunks])
+    first = load(table_hbm, table_ref, sems.at[2])
+    halves = [pl.ds(h * SLABS, SLABS) for h in range(2)]
     copies = [
-        load(field_hbm.at[chunk(i)], field_ref.at[chunk(i)], sems.at[i]) for i in range(chunks)
+        load(field_hbm.at[at], field_ref.at[at], sems.at[h]) for h, at in enumerate(halves)
     ]
     first.wait()
     parts = []
-    for i in range(chunks):
-        copies[i].wait()
-        parts.append(dot(flat(field_ref[i * CHUNK : (i + 1) * CHUNK]), table_ref[...]))
-    per_half = SLABS // CHUNK
+    for h, at in enumerate(halves):
+        copies[h].wait()
+        parts.append(dot(flat(field_ref[at]), table_ref[...]))
     for h in range(2):
-        pack(jnp.concatenate(parts[h * per_half : (h + 1) * per_half], axis=0), out_ref, h)
+        pack(parts[h], out_ref, h)
 
 
 def middle_kernel(
@@ -267,7 +266,7 @@
     out_ref[...] = dot(mixed, order_t_ref[...]).astype(BF16)
 
 
-def grad_kernel(spec_ref, dmixed_ref, order_ref, after_hbm, early_ref, out_ref):
+def grad_kernel(spec_ref, dmixed_ref, order_ref, early_ref, out_ref):
     spec = dot(spec_ref[...], order_ref[...])
     dmixed = dot(dmixed_ref[...], order_ref[...]).astype(BF16)
     rows = spec.shape[0]
@@ -359,7 +358,7 @@
     sent = call(
         row_in_kernel, shaped(sent_shape), "row_in", 60,
         in_specs=[HBM] * 2, out_specs=WHOLE,
-        scratch_shapes=buffers(field_shape, tall) + [sems(chunks + 1)],
+        scratch_shapes=buffers(field_shape, tall) + [sems(3)],
     )(field, turned(row_fwd_t))
     arrived = across(sent, "pencil").reshape(height, wide)
     modes = column(fwd_table, arrived, "column_in", weights)
@@ -373,18 +372,21 @@
     )(field, cot, back.reshape(sent_shape), inv_table)
     arrived = across(sent, "pencil").reshape(height, wide)
     dmixed = across(column(turned(col_inv), arrived, "column_in_t"), "dp")
-    sent = column(turned(col_fwd), mix(dmixed, True, "mix_t"), "column_out_t")
-    back = across(sent, "pencil").reshape(sent_shape)
+    dspectrum = mix(dmixed, True, "mix_t")
     grad_weight = call(
         grad_kernel, shaped((GROUP, GROUP, channels, 2 * channels), F32), "weight_grad",
-        in_specs=[WHOLE] * 3 + [HBM, WHOLE], out_specs=WHOLE,
-    )(spectrum, dmixed, order_in, sent, row_table)
+    )(spectrum, dmixed, order_in, row_table).reshape(spectral_weight.shape)
+    sent = call(
+        column_kernel, shaped((height, wide)), "column_out_t",
+        in_specs=[WHOLE, WHOLE, HBM], out_specs=WHOLE,
+    )(turned(col_fwd), dspectrum, grad_weight)
+    back = across(sent, "pencil").reshape(sent_shape)
     grad_input = call(
         row_out_kernel, shaped(field_shape), "row_out", 52,
         in_specs=[HBM, WHOLE, WHOLE], out_specs=HBM,
         scratch_shapes=buffers(field_shape, field_shape) + [sems(chunks)] * 2,
     )(dpre, back, row_table)
-    return (grad_input[None], grad_weight.reshape(spectral_weight.shape))
+    return (grad_input[None], grad_weight)
 
 
 def solution(mesh):

time: 159 us -> 160 us (level)
  blocking collectives: 82.9 us -> 95.3 us
  waiting for transfers between devices: 24.2 us -> 15.3 us
  starting transfers between devices: 16.6 us -> 14.6 us
    all_to_all x6, blocking collectives: 82.9 us -> 95.3 us  [across(): return lax.all_to_all(values, axis, split_axis=0, concat_axis=0, tiled=True)]
    all_to_all x2, waiting for transfers between devices: 24.2 us -> 15.3 us  [across(): return lax.all_to_all(values, axis, split_axis=0, concat_axis=0, tiled=True)]
    all_to_all x2, starting transfers between devices: 16.6 us -> 14.6 us  [across(): return lax.all_to_all(values, axis, split_axis=0, concat_axis=0, tiled=True)]
    unnamed x26 -> x28, local copies, waits for them, and re-layouts: 3.23 us -> 4.27 us
  transfers between devices with their start and end apart: 2 -> 2, of which waited for: 2 -> 2; matrix products, arithmetic and copies ran while one was open for 2% -> 1% of each run, Pallas kernels for 3% -> 3%
where the time goes in v4:
time: 160 us; the launch traced here: 159 us
  blocking collectives  95.3 us (60%)
  Pallas kernels  27.3 us (17%)
  waiting for transfers between devices  15.3 us (10%)
  starting transfers between devices  14.6 us (9%)
  local copies, waits for them, and re-layouts  5.95 us (4%)
    all_to_all x6, blocking collectives, across(): return lax.all_to_all(values, axis, split_axis=0, concat_axis=0, tiled=True)  95.3 us
    all_to_all x2, waiting for transfers between devices, across(): return lax.all_to_all(values, axis, split_axis=0, concat_axis=0, tiled=True)  15.3 us
    all_to_all x2, starting transfers between devices, across(): return lax.all_to_all(values, axis, split_axis=0, concat_axis=0, tiled=True)  14.6 us
    pallas_call x1, Pallas kernels, local(): call(middle_kernel, [shaped(field_shape), shaped(sent_shape)], 'middle',...  8.47 us
    pallas_call x1, Pallas kernels, local(): call(row_in_kernel, shaped(sent_shape), 'row_in', 60, in_specs=[HBM] * 2,...  5.57 us
    unnamed x28, local copies, waits for them, and re-layouts  4.27 us
    pallas_call x1, Pallas kernels, local(): call(row_out_kernel, shaped(field_shape), 'row_out', 52, in_specs=[HBM, W...  4.19 us
  transfers between devices with their start and end apart: 2, of which 2 were waited for; matrix products, arithmetic and copies ran while one was open for 1% of the time, Pallas kernels for 3%

profile of v4, /device:TPU:32, one launch (start us, length us, event | category | flops | bytes accessed | tf_op | source)
XLA Modules:
  0.0 159.3 jit_solution(16912750956593495798)
XLA Ops:
  0.6 0.0 copy-start.1
  0.6 0.0 copy-start.2
  0.7 0.0 copy-start.13
  0.7 5.6 %row_in.1 = bf16[16,32,512]{2,1,0:T(8,128)(2,1)} custom-call(bf16[32,32,2048]{2,1,0:T(8,128)(2,1)} %bitcast.17, bf16[2048,256]{1,0:T(8,128)(2,1)} %constant.24.clone.table_hbm), custom_call_target="tpu_custom_call" | custom-call | tf_op jit(solution)/shard_map/row_in/pallas_call | solution.py:358
  6.2 11.1 %all-to-all-start = ((bf16[16,32,512]{2,1,0:T(8,128)(2,1)}), bf16[16,32,512]{2,1,0:T(8,128)(2,1)}, u32[]{:S(2)}, u32[]{:S(2)}) async-start(bf16[16,32,512]{2,1,0:T(8,128)(2,1)} %row_in.1), calls=%async_computation | async-start | bytes 1048576 | tf_op jit(solution)/shard_map/all_to_all | solution.py:315
  17.3 0.0 copy-done.13
  17.3 1.3 reshape.33.in_ref
  18.6 0.0 copy-done.1
  18.6 0.0 copy-done.2
  18.6 0.0 copy-start.7
  18.6 1.0 copy-done.7
  19.7 1.0 copy-done.9
  20.7 0.0 copy-start.3
  20.7 2.1 %weight_blocks.1.early_and_out_0_.weight_ref = bf16[4,128,1024]{2,1,0:T(8,128)(2,1)S(1)} custom-call(bf16[8,8,32,64]{3,2,1,0:T(8,128)(2,1)S(1)} %copy-done.9, bf16[512,512]{1,0:T(8,128)(2,1)S(1)} %copy-done.1, bf16[512,512]{1,0:T(8,128)(2,1)S(1)} %copy-done.2, bf16[1024,256]{1,0:T(8,128)(2,1)S(1)} %copy-done.7), custom_call_target="tpu_custom_call" | custom-call | tf_op jit(solution)/shard_map/weight_blocks/pallas_call | solution.py:346
  22.8 10.9 %all-to-all-done = bf16[16,32,512]{2,1,0:T(8,128)(2,1)} async-done(((bf16[16,32,512]{2,1,0:T(8,128)(2,1)}), bf16[16,32,512]{2,1,0:T(8,128)(2,1)}, u32[]{:S(2)}, u32[]{:S(2)}) %all-to-all-start) | async-done | bytes 524320 | tf_op jit(solution)/shard_map/all_to_all | solution.py:315
  33.7 0.0 copy-start.8
  33.7 0.0 copy-start.10
  33.7 1.1 copy-done.10
  34.8 0.0 copy-start
  34.8 1.5 column_in.1
  36.3 11.1 %all_to_all.72 = bf16[16,8,512]{2,1,0:T(8,128)(2,1)S(1)} all-to-all(bf16[16,8,512]{2,1,0:T(8,128)(2,1)S(1)} %bitcast.26), channel_id=1, replica_groups=mesh['dp'=16,'pencil'=16] {'dp'}, dimensions={0} | all-to-all | bytes 262144 | tf_op jit(solution)/shard_map/all_to_all | solution.py:315
  47.5 0.8 mix.1
  48.3 9.3 %all_to_all.73 = bf16[16,8,512]{2,1,0:T(8,128)(2,1)S(1)} all-to-all(bf16[16,8,512]{2,1,0:T(8,128)(2,1)S(1)} %bitcast.29), channel_id=1, replica_groups=mesh['dp'=16,'pencil'=16] {'dp'}, dimensions={0} | all-to-all | bytes 262144 | tf_op jit(solution)/shard_map/all_to_all | solution.py:315
  57.6 0.0 copy-done.3
  57.6 0.0 copy-done.8
  57.6 0.3 column_out.1
  57.9 22.1 %all_to_all.74.back_ref = bf16[16,32,512]{2,1,0:T(8,128)(2,1)S(1)} all-to-all(bf16[16,32,512]{2,1,0:T(8,128)(2,1)S(1)} %bitcast.19), channel_id=1, replica_groups=mesh['dp'=16,'pencil'=16] {'pencil'}, dimensions={0} | all-to-all | bytes 1048576 | tf_op jit(solution)/shard_map/all_to_all | solution.py:315
  80.0 0.0 copy-done
  80.0 8.5 %middle.1 = (bf16[32,32,2048]{2,1,0:T(8,128)(2,1)S(1)}, bf16[16,32,512]{2,1,0:T(8,128)(2,1)S(1)}) custom-call(bf16[32,32,2048]{2,1,0:T(8,128)(2,1)S(1)} %bitcast.18, bf16[32,32,2048]{2,1,0:T(8,128)(2,1)} %bitcast.31, bf16[16,32,512]{2,1,0:T(8,128)(2,1)S(1)} %all_to_all.74.back_ref, bf16[256,2048]{1,0:T(8,128)(2,1)S(1)} %copy-done.3), custom_call_target="tpu_custom_call" | custom-call | tf_op jit(solution)/shard_map/middle/pallas_call | solution.py:368
  88.5 0.0 copy-start.4
  88.5 0.0 copy-start.5
  88.5 21.4 %all_to_all.75 = bf16[16,32,512]{2,1,0:T(8,128)(2,1)S(1)} all-to-all(bf16[16,32,512]{2,1,0:T(8,128)(2,1)S(1)} %get-tuple-element.5), channel_id=1, replica_groups=mesh['dp'=16,'pencil'=16] {'pencil'}, dimensions={0} | all-to-all | bytes 1048576 | tf_op jit(solution)/shard_map/all_to_all | solution.py:315
  110.0 0.0 copy-done.12
  110.0 0.3 column_in_t.1
  110.3 9.6 %all_to_all.76 = bf16[16,8,512]{2,1,0:T(8,128)(2,1)S(1)} all-to-all(bf16[16,8,512]{2,1,0:T(8,128)(2,1)S(1)} %bitcast.28), channel_id=1, replica_groups=mesh['dp'=16,'pencil'=16] {'dp'}, dimensions={0} | all-to-all | bytes 262144 | tf_op jit(solution)/shard_map/all_to_all | solution.py:315
  119.8 1.8 %mix_t.1 = bf16[128,512]{1,0:T(8,128)(2,1)} custom-call(bf16[128,512]{1,0:T(8,128)(2,1)S(1)} %bitcast.24, bf16[4,128,1024]{2,1,0:T(8,128)(2,1)S(1)} %weight_blocks.1.early_and_out_0_.weight_ref, bf16[512,512]{1,0:T(8,128)(2,1)S(1)} %copy-done.1, bf16[512,512]{1,0:T(8,128)(2,1)S(1)} %copy-done.2), custom_call_target="tpu_custom_call" | custom-call | tf_op jit(solution)/shard_map/mix_t/pallas_call | solution.py:355
  121.7 0.0 copy-done.4
  121.7 3.5 %all-to-all-start.6 = ((bf16[16,8,512]{2,1,0:T(8,128)(2,1)}), bf16[16,8,512]{2,1,0:T(8,128)(2,1)S(1)}, u32[]{:S(2)}, u32[]{:S(2)}) async-start(bf16[16,8,512]{2,1,0:T(8,128)(2,1)} %bitcast.11), calls=%async_computation.6 | async-start | bytes 262144 | tf_op jit(solution)/shard_map/all_to_all | solution.py:315
  125.2 0.0 copy-done.5
  125.2 2.0 %weight_grad.1 = f32[8,8,32,64]{3,2,1,0:T(8,128)S(1)} custom-call(bf16[128,512]{1,0:T(8,128)(2,1)S(1)} %bitcast.23, bf16[128,512]{1,0:T(8,128)(2,1)S(1)} %bitcast.25, bf16[512,512]{1,0:T(8,128)(2,1)S(1)} %copy-done.1, bf16[256,2048]{1,0:T(8,128)(2,1)S(1)} %copy-done.5), custom_call_target="tpu_custom_call" | custom-call | tf_op jit(solution)/shard_map/weight_grad/pallas_call | solution.py:376
  127.2 0.4 reshape.35.early_and_out_0_
  127.5 0.0 copy-start.6
  127.5 4.3 %all-to-all-done.6 = bf16[16,8,512]{2,1,0:T(8,128)(2,1)S(1)} async-done(((bf16[16,8,512]{2,1,0:T(8,128)(2,1)}), bf16[16,8,512]{2,1,0:T(8,128)(2,1)S(1)}, u32[]{:S(2)}, u32[]{:S(2)}) %all-to-all-start.6) | async-done | bytes 131104 | tf_op jit(solution)/shard_map/all_to_all | solution.py:315
  131.9 1.0 copy-done.11
  132.9 0.3 column_out_t.1
  133.2 21.7 %all_to_all.77.back_ref = bf16[16,32,512]{2,1,0:T(8,128)(2,1)S(1)} all-to-all(bf16[16,32,512]{2,1,0:T(8,128)(2,1)S(1)} %bitcast.21), channel_id=1, replica_groups=mesh['dp'=16,'pencil'=16] {'pencil'}, dimensions={0} | all-to-all | bytes 1048576 | tf_op jit(solution)/shard_map/all_to_all | solution.py:315
  154.9 4.2 %row_out.1 = bf16[32,32,2048]{2,1,0:T(8,128)(2,1)} custom-call(bf16[32,32,2048]{2,1,0:T(8,128)(2,1)} %copy-done.4, bf16[16,32,512]{2,1,0:T(8,128)(2,1)S(1)} %all_to_all.77.back_ref, bf16[256,2048]{1,0:T(8,128)(2,1)S(1)} %copy-done.5), custom_call_target="tpu_custom_call" | custom-call | tf_op jit(solution)/shard_map/row_out/pallas_call | solution.py:384
  159.1 0.0 copy-done.6
  (3 shorter events, 0.0 us)
Async XLA Ops:
  0.6 18.0 %copy-start.1 = (bf16[512,512]{1,0:T(8,128)(2,1)S(1)}, bf16[512,512]{1,0:T(8,128)(2,1)}, u32[]{:S(2)}) copy-start(bf16[512,512]{1,0:T(8,128)(2,1)} %constant.20.clone.early_and_out_0_.order_ref) | copy-start | bytes 1572868
  0.6 18.0 %copy-start.2 = (bf16[512,512]{1,0:T(8,128)(2,1)S(1)}, bf16[512,512]{1,0:T(8,128)(2,1)}, u32[]{:S(2)}) copy-start(bf16[512,512]{1,0:T(8,128)(2,1)} %constant.21.clone.early_and_out_1_.order_t_ref) | copy-start | bytes 1572868
  0.7 16.6 %copy-start.13 = (bf16[8,8,2048]{2,1,0:T(8,128)(2,1)S(1)}, bf16[8,8,2048]{2,1,0:T(8,128)(2,1)}, u32[]{:S(2)}) copy-start(bf16[8,8,2048]{2,1,0:T(8,128)(2,1)} %param.14) | copy-start | bytes 786436
  6.2 27.5 %all-to-all-start = ((bf16[16,32,512]{2,1,0:T(8,128)(2,1)}), bf16[16,32,512]{2,1,0:T(8,128)(2,1)}, u32[]{:S(2)}, u32[]{:S(2)}) async-start(bf16[16,32,512]{2,1,0:T(8,128)(2,1)} %row_in.1), calls=%async_computation | async-start | bytes 1048576 | tf_op jit(solution)/shard_map/all_to_all | solution.py:315
  18.6 1.0 copy-start.7
  19.7 1.0 copy-start.9
  20.7 36.9 %copy-start.3 = (bf16[256,2048]{1,0:T(8,128)(2,1)S(1)}, bf16[256,2048]{1,0:T(8,128)(2,1)}, u32[]{:S(2)}) copy-start(bf16[256,2048]{1,0:T(8,128)(2,1)} %constant.18.clone.early_and_out_0_.inv_ref) | copy-start | bytes 3145732
  33.7 23.9 %copy-start.8 = (bf16[1024,256]{1,0:T(8,128)(2,1)S(1)}, bf16[1024,256]{1,0:T(8,128)(2,1)}, u32[]{:S(2)}) copy-start(bf16[1024,256]{1,0:T(8,128)(2,1)} %constant.23.clone.early_and_out_2_.table_ref) | copy-start | bytes 1572868
  33.7 1.1 copy-start.10
  34.8 45.2 %copy-start = (bf16[1,32,32,2048]{3,2,1,0:T(8,128)(2,1)S(1)}, bf16[1,32,32,2048]{3,2,1,0:T(8,128)(2,1)}, u32[]{:S(2)}) copy-start(bf16[1,32,32,2048]{3,2,1,0:T(8,128)(2,1)} %param.12) | copy-start | bytes 12582916
  80.0 30.0 %copy-start.12 = (bf16[256,1024]{1,0:T(8,128)(2,1)S(1)}, bf16[256,1024]{1,0:T(8,128)(2,1)}, u32[]{:S(2)}) copy-start(bf16[256,1024]{1,0:T(8,128)(2,1)} %constant.25.clone.table_ref) | copy-start | bytes 1572868
  88.5 33.2 %copy-start.4 = (bf16[32,32,2048]{2,1,0:T(8,128)(2,1)}, bf16[32,32,2048]{2,1,0:T(8,128)(2,1)S(1)}, u32[]{:S(2)}) copy-start(bf16[32,32,2048]{2,1,0:T(8,128)(2,1)S(1)} %get-tuple-element.4.dpre_hbm) | copy-start | bytes 12582916
  88.5 36.7 %copy-start.5 = (bf16[256,2048]{1,0:T(8,128)(2,1)S(1)}, bf16[256,2048]{1,0:T(8,128)(2,1)}, u32[]{:S(2)}) copy-start(bf16[256,2048]{1,0:T(8,128)(2,1)} %constant.19.clone.early_ref.table_ref) | copy-start | bytes 3145732
  121.7 10.2 %all-to-all-start.6 = ((bf16[16,8,512]{2,1,0:T(8,128)(2,1)}), bf16[16,8,512]{2,1,0:T(8,128)(2,1)S(1)}, u32[]{:S(2)}, u32[]{:S(2)}) async-start(bf16[16,8,512]{2,1,0:T(8,128)(2,1)} %bitcast.11), calls=%async_computation.6 | async-start | bytes 262144 | tf_op jit(solution)/shard_map/all_to_all | solution.py:315
  127.5 31.6 %copy-start.6 = (f32[8,8,2048]{2,1,0:T(8,128)}, f32[8,8,2048]{2,1,0:T(8,128)S(1)}, u32[]{:S(2)}) copy-start(f32[8,8,2048]{2,1,0:T(8,128)S(1)} %reshape.35.early_and_out_0_) | copy-start | bytes 1572868
  131.9 1.0 copy-start.11
